TPU v7x, 512 devices: a whole 4x4x16 slice. The times are simulated.
512 devices in a mesh: section: 8 (over x_hi, y), tensor: 16 (over z), dp: 4 (over x_lo, core).
Axes of the slice: x: 4 (x_hi: 2, x_lo: 2; x = x_hi * 2 + x_lo), y: 4, z: 16, core: 2. Of those that a mesh axis runs over, the one named last changes fastest.
Arguments:
- activations: bfloat16 [512, 8, 8192], P('tensor', 'dp', 'section'), may hold values from -6 to 6
- old_heads: int32 [128], replicated, may hold values from 0 to 127, as said below
- new_heads: int32 [128], replicated, may hold values from 0 to 127, as said below
- xz_weight: bfloat16 [8192, 128, 128], P(('section', 'dp'), 'tensor'), may hold values from -0.0625 to 0.0625
- dt_weight: bfloat16 [8192, 128], P(('section', 'dp'), 'tensor'), may hold values from -0.0625 to 0.0625
- bc_weight: bfloat16 [8192, 2048], P('section', 'tensor'), may hold values from -0.0625 to 0.0625
- conv_heads: bfloat16 [128, 4, 64], P('tensor'), may hold values from -2.5 to 2.5
- conv_groups: bfloat16 [4, 2048], P(None, 'tensor'), may hold values from -2.5 to 2.5
- decay_log: bfloat16 [128], P('tensor'), may hold values from -5.5 to 1
- dt_bias: bfloat16 [128], P('tensor'), may hold values from -6 to -4
- skip_gain: bfloat16 [128], P('tensor'), may hold values from 0.5 to 1.5
- norm_gain: bfloat16 [128, 64], P('tensor'), may hold values from 0.5 to 1.5
- out_weight: bfloat16 [128, 64, 8192], P('tensor', None, ('section', 'dp')), may hold values from -0.0625 to 0.0625
Outputs:
- mixed: bfloat16 [512, 8, 8192], P(None, 'dp', 'section')
- relaid_xz: bfloat16 [8192, 128, 128], P(('section', 'dp'), 'tensor')
- relaid_out: bfloat16 [128, 64, 8192], P('tensor', None, ('section', 'dp'))
Inputs may be any that keep to these rules, and one draw needn't show every extreme that they name: `old_heads`: a permutation of the head numbers. `new_heads`: a permutation of the head numbers; the heads of the old slots d * 8 .. (d+1) * 8 - 1 and of the new slots e * 8 .. (e+1) * 8 - 1 have at most 1 in common for any d and e, and exactly 1 for some pairs.
All inputs are finite; a program needn't handle non-finite values.
Results may differ from a plain program's by a relative error of at most 0.027.
Values may be sent and summed in bfloat16 or wider, within the bound.
A program may use at most 64 MiB of HBM per device.

v0:
```python
import jax
import jax.numpy as jnp
from jax import lax
from jax.sharding import PartitionSpec as P

STATE = 256
GROUP_HEADS = 32
KERNEL = 4


def passed_along(value, axis, by):
    peers = lax.axis_size(axis)
    pairs = [(i, i + by) for i in range(peers) if 0 <= i + by < peers]
    return lax.ppermute(value, axis, pairs)


def for_sending(value):

    def short(part):
        return part.astype(jnp.bfloat16) if part.dtype == jnp.float32 else part

    return jax.tree.map(short, value)


def per_device(
    activations,
    old_heads,
    new_heads,
    xz_weight,
    dt_weight,
    bc_weight,
    conv_heads,
    conv_groups,
    decay_log,
    dt_bias,
    skip_gain,
    norm_gain,
    out_weight,
):
    owners = lax.axis_size("tensor")
    member = lax.axis_index("tensor")
    sections = lax.axis_size("section")
    head_dev = xz_weight.shape[1]
    head_size = xz_weight.shape[2] // 2
    total_heads = old_heads.shape[0]
    capacity = max(1, head_dev // owners)
    highest = lax.Precision.HIGHEST
    mine_old = lax.dynamic_slice_in_dim(old_heads, member * head_dev, head_dev)
    mine_new = lax.dynamic_slice_in_dim(new_heads, member * head_dev, head_dev)
    numbers = jnp.arange(total_heads, dtype=jnp.int32)
    position = jnp.sum(
        jnp.where(new_heads[None, :] == mine_old[:, None], numbers[None, :], 0), axis=1
    )
    target = position // head_dev
    new_slot = position % head_dev
    indices = jnp.arange(head_dev, dtype=jnp.int32)
    earlier = (target[:, None] == target[None, :]) & (indices[:, None] < indices[None, :])
    order_rank = jnp.sum(earlier.astype(jnp.int32), axis=0)
    chosen = (target[None, None, :] == jnp.arange(owners, dtype=jnp.int32)[:, None, None]) & (
        order_rank[None, None, :] == jnp.arange(capacity, dtype=jnp.int32)[None, :, None]
    )
    chosen_mask = chosen.astype(jnp.bfloat16)
    slot_hot = (new_slot[:, None] == indices[None, :]).astype(jnp.bfloat16)
    params = jnp.stack([decay_log, dt_bias, skip_gain], axis=1)

    def select(form, array):
        return jnp.einsum(form, chosen_mask, array, preferred_element_type=jnp.float32).astype(
            jnp.bfloat16
        )

    sending = (
        select("dcj,jk->dck", slot_hot),
        select("dcj,rjq->dcrq", xz_weight),
        select("dcj,rj->dcr", dt_weight),
        select("dcj,jer->dcer", out_weight),
        select("dcj,jwe->dcwe", conv_heads),
        select("dcj,jp->dcp", params),
        select("dcj,je->dce", norm_gain),
    )
    received = (
        lax.all_to_all(sending[0], "tensor", split_axis=0, concat_axis=0, tiled=True),
        lax.all_to_all(sending[1], "tensor", split_axis=0, concat_axis=0, tiled=True),
        lax.all_to_all(sending[2], "tensor", split_axis=0, concat_axis=0, tiled=True),
        lax.all_to_all(sending[3], "tensor", split_axis=0, concat_axis=0, tiled=True),
        lax.all_to_all(sending[4], "tensor", split_axis=0, concat_axis=0, tiled=True),
        lax.all_to_all(sending[5], "tensor", split_axis=0, concat_axis=0, tiled=True),
        lax.all_to_all(sending[6], "tensor", split_axis=0, concat_axis=0, tiled=True),
    )
    placing = received[0]

    def place(form, array):
        return jnp.einsum(form, placing, array, preferred_element_type=jnp.float32).astype(
            jnp.bfloat16
        )

    new_xz = place("sck,scrq->rkq", received[1])
    new_dt = place("sck,scr->rk", received[2])
    new_out = place("sck,scer->ker", received[3])
    new_conv = place("sck,scwe->kwe", received[4])
    new_params = place("sck,scp->kp", received[5])
    new_gain = place("sck,sce->ke", received[6])
    full_xz, full_dt, full_out = (
        lax.all_gather(new_xz, "dp", axis=0, tiled=True),
        lax.all_gather(new_dt, "dp", axis=0, tiled=True),
        lax.all_gather(new_out, "dp", axis=2, tiled=True),
    )
    conv_here, param_here, gain_here, heads_here = (new_conv, new_params, new_gain, mine_new)
    gathered = lax.all_gather(activations, "tensor", axis=0, tiled=True)
    seq_len, micro, width = gathered.shape
    flattened = gathered.reshape(seq_len * micro, width)
    inner = head_dev * head_size
    big_weight = jnp.concatenate([full_xz.reshape(width, 2 * inner), bc_weight], axis=1)
    proj_big, proj_step = jax.tree.map(
        lambda part: lax.psum_scatter(
            part.astype(jnp.bfloat16), "section", scatter_dimension=0, tiled=True
        ).astype(jnp.float32),
        (
            jnp.dot(flattened, big_weight, preferred_element_type=jnp.float32),
            jnp.dot(flattened, full_dt, preferred_element_type=jnp.float32),
        ),
    )
    tokens = seq_len // sections
    proj_big = proj_big.reshape(tokens, micro, proj_big.shape[1])
    xz_proj = proj_big[..., : 2 * inner].reshape(tokens, micro, head_dev, 2 * head_size)
    conv_in = jnp.concatenate(
        [xz_proj[..., :head_size].reshape(tokens, micro, inner), proj_big[..., 2 * inner :]], axis=2
    )
    rim_rows = passed_along(conv_in[tokens - (KERNEL - 1) :], "section", 1)
    extended = jnp.concatenate([rim_rows, conv_in], axis=0)
    kernel = jnp.concatenate(
        [
            jnp.transpose(conv_here.astype(jnp.float32), (1, 0, 2)).reshape(KERNEL, inner),
            conv_groups.astype(jnp.float32),
        ],
        axis=1,
    )
    conv_sum = jnp.zeros_like(conv_in)
    for offset in range(KERNEL):
        conv_sum = conv_sum + kernel[offset] * extended[offset : offset + tokens]
    convolved = jax.nn.silu(conv_sum).astype(jnp.bfloat16)
    x_values = (
        convolved[..., :inner].astype(jnp.float32).reshape(tokens, micro, head_dev, head_size)
    )
    bc_all = lax.all_gather(convolved[..., inner:], "tensor", axis=2, tiled=True)
    groups = bc_all.shape[2] // (2 * STATE)
    bc_all = bc_all.reshape(tokens, micro, 2, groups, STATE)
    group_hot = (
        heads_here[:, None] // GROUP_HEADS == jnp.arange(groups, dtype=jnp.int32)[None, :]
    ).astype(jnp.bfloat16)
    b_heads = jnp.einsum(
        "tmgs,hg->tmhs", bc_all[:, :, 0], group_hot, preferred_element_type=jnp.float32
    )
    c_heads = jnp.einsum(
        "tmgs,hg->tmhs", bc_all[:, :, 1], group_hot, preferred_element_type=jnp.float32
    )
    step_size = jax.nn.softplus(
        proj_step.reshape(tokens, micro, head_dev) + param_here[:, 1].astype(jnp.float32)
    )
    log_decay = -step_size * jnp.exp(param_here[:, 0].astype(jnp.float32))
    cumulative = jnp.cumsum(log_decay, axis=0)
    moved = jnp.transpose(cumulative, (1, 2, 0))
    causal = jnp.arange(tokens)[:, None] >= jnp.arange(tokens)[None, :]
    spread = jnp.where(causal, moved[:, :, :, None] - moved[:, :, None, :], -jnp.inf)
    weighting = jnp.exp(spread) * jnp.transpose(step_size, (1, 2, 0))[:, :, None, :]
    scores = jnp.einsum("tmhn,smhn->mhts", c_heads, b_heads, precision=highest)
    y_inside = jnp.einsum("mhts,smhe->tmhe", scores * weighting, x_values, precision=highest)
    block_end = cumulative[tokens - 1]
    tail_weight = jnp.exp(block_end[None] - cumulative) * step_size
    local_state = jnp.einsum(
        "tmh,tmhe,tmhn->mhen", tail_weight, x_values, b_heads, precision=highest
    )
    local_decay = jnp.exp(block_end)
    incoming = jnp.zeros_like(local_state)
    for turn in range(sections - 1):
        incoming = passed_along(
            for_sending(local_decay[:, :, None, None] * incoming + local_state), "section", 1
        )
    y_carry = jnp.exp(cumulative)[..., None] * jnp.einsum(
        "tmhn,mhen->tmhe", c_heads, incoming, precision=highest
    )
    y_values = y_inside + y_carry + param_here[:, 2].astype(jnp.float32)[:, None] * x_values
    gated = y_values * jax.nn.silu(xz_proj[..., head_size:])
    head_squares = jnp.sum(gated * gated, axis=3)
    group_float = group_hot.astype(jnp.float32)
    group_squares = jnp.einsum("tmh,hg->tmg", head_squares, group_float, precision=highest)
    group_squares = lax.psum(group_squares, "tensor")
    inverse = lax.rsqrt(group_squares / (GROUP_HEADS * head_size) + 1e-05)
    head_scale = jnp.einsum("tmg,hg->tmh", inverse, group_float, precision=highest)
    normed = (
        (gated * head_scale[..., None] * gain_here.astype(jnp.float32))
        .astype(jnp.bfloat16)
        .reshape(tokens, micro, inner)
    )
    out_rows = full_out.reshape(inner, width)
    piece = lax.all_gather(normed, "section", axis=0, tiled=True)
    product = jnp.dot(
        piece.reshape(piece.shape[0] * piece.shape[1], inner),
        out_rows,
        preferred_element_type=jnp.float32,
    )
    partial_sum = product.reshape(piece.shape[0], piece.shape[1], width)
    total = lax.psum(partial_sum.astype(jnp.bfloat16), "tensor").astype(jnp.float32)
    mixed = (gathered.astype(jnp.float32) + total).astype(jnp.bfloat16)
    return (mixed, new_xz, new_out)


def solution(mesh):
    in_specs = (
        P("tensor", "dp", "section"),
        P(),
        P(),
        P(("section", "dp"), "tensor", None),
        P(("section", "dp"), "tensor"),
        P("section", "tensor"),
        P("tensor", None, None),
        P(None, "tensor"),
        P("tensor"),
        P("tensor"),
        P("tensor"),
        P("tensor", None),
        P("tensor", None, ("section", "dp")),
    )
    out_specs = (
        P(None, "dp", "section"),
        P(("section", "dp"), "tensor", None),
        P("tensor", None, ("section", "dp")),
    )
    return jax.shard_map(
        per_device, mesh=mesh, in_specs=in_specs, out_specs=out_specs, check_vma=False
    )
```

profile of v0, /device:TPU:6, one launch (start us, length us, event | category | flops | bytes accessed | tf_op | source)
XLA Modules:
  0.0 791.9 jit_solution(2064027406477446982)
XLA Ops:
  9.9 15.2 %all-to-all-start = ((bf16[16,1,8]{2,1,0:T(2,128)(2,1)}), bf16[16,1,8]{2,1,0:T(2,128)(2,1)S(1)}, u32[]{:S(2)}, u32[]{:S(2)}) async-start(bf16[16,1,8]{2,1,0:T(2,128)(2,1)} %copy.167), calls=%async_computation | async-start | bytes 16384 | tf_op jit(solution)/shard_map/all_to_all | solution.py:81
  26.9 10.5 %all-to-all-done = bf16[16,1,8]{2,1,0:T(2,128)(2,1)S(1)} async-done(((bf16[16,1,8]{2,1,0:T(2,128)(2,1)}), bf16[16,1,8]{2,1,0:T(2,128)(2,1)S(1)}, u32[]{:S(2)}, u32[]{:S(2)}) %all-to-all-start) | async-done | bytes 288 | tf_op jit(solution)/shard_map/all_to_all | solution.py:81
  37.4 3.7 all-to-all-start.2
  42.0 54.3 %all-to-all-done.2 = bf16[16,1,256,128]{3,2,1,0:T(8,128)(2,1)S(1)} async-done(((bf16[16,1,256,128]{3,2,1,0:T(8,128)(2,1)}), bf16[16,1,256,128]{3,2,1,0:T(8,128)(2,1)S(1)}, u32[]{:S(2)}, u32[]{:S(2)}) %all-to-all-start.2) | async-done | bytes 1048608 | tf_op jit(solution)/shard_map/all_to_all | solution.py:82
  99.3 19.8 %all_to_all.35 = bf16[16,2,128]{2,1,0:T(2,128)(2,1)S(1)} all-to-all(bf16[16,2,128]{2,1,0:T(2,128)(2,1)S(1)} %reshape.324), channel_id=1, replica_groups=mesh['section'=8,'tensor'=16,'dp'=4] {'tensor'}, dimensions={0} | all-to-all | bytes 16384 | tf_op jit(solution)/shard_map/all_to_all | solution.py:83
  119.2 5.2 all_gather.21
  124.4 10.5 %all-gather.5.cloned.1.call-done = bf16[512,2,1024]{2,0,1:T(8,128)(2,1)} async-done(((bf16[32,2,1024]{2,0,1:T(8,128)(2,1)}), bf16[512,2,1024]{2,0,1:T(8,128)(2,1)}) %all-gather.5.cloned.1.call-update) | async-done | bytes 2097168 | tf_op jit(solution)/shard_map/all_gather | solution.py:108
  134.9 5.1 copy.174
  144.3 25.5 %all-gather.7.cloned.1.call-done = bf16[1024,8,128]{2,1,0:T(8,128)(2,1)} async-done(((bf16[256,8,128]{2,1,0:T(8,128)(2,1)}), bf16[1024,8,128]{2,1,0:T(8,128)(2,1)}) %all-gather.7.cloned.1.call-update) | async-done | bytes 2097168 | tf_op jit(solution)/shard_map/all_gather | solution.py:103
  172.1 4.0 fusion
  176.0 4.3 copy.205
  181.9 12.3 %all-to-all-start.4 = ((bf16[16,1,3]{2,1,0:T(2,128)(2,1)}), bf16[16,1,3]{2,1,0:T(2,128)(2,1)S(1)}, u32[]{:S(2)}, u32[]{:S(2)}) async-start(bf16[16,1,3]{2,1,0:T(2,128)(2,1)} %copy.186), calls=%async_computation.4 | async-start | bytes 16384 | tf_op jit(solution)/shard_map/all_to_all | solution.py:86
  195.2 11.4 %all-to-all-done.4 = bf16[16,1,3]{2,1,0:T(2,128)(2,1)S(1)} async-done(((bf16[16,1,3]{2,1,0:T(2,128)(2,1)}), bf16[16,1,3]{2,1,0:T(2,128)(2,1)S(1)}, u32[]{:S(2)}, u32[]{:S(2)}) %all-to-all-start.4) | async-done | bytes 128 | tf_op jit(solution)/shard_map/all_to_all | solution.py:86
  210.3 12.1 %all-to-all-done.1 = bf16[16,2,128]{2,1,0:T(2,128)(2,1)S(1)} async-done(((bf16[16,2,128]{2,1,0:T(2,128)(2,1)}), bf16[16,2,128]{2,1,0:T(2,128)(2,1)S(1)}, u32[]{:S(2)}, u32[]{:S(2)}) %all-to-all-start.1) | async-done | bytes 8224 | tf_op jit(solution)/shard_map/all_to_all | solution.py:85
  222.7 38.3 %reduce-scatter.9.cloned.1.call-done = bf16[128,8]{1,0:T(8,128)(2,1)} async-done(((bf16[1024,8]{1,0:T(8,128)(2,1)}), bf16[128,8]{1,0:T(8,128)(2,1)}) %reduce-scatter.9.cloned.1.call-update) | async-done | bytes 2064
  262.5 93.4 %reduce-scatter.7.cloned.1.call-done = bf16[128,1152]{1,0:T(8,128)(2,1)} async-done(((bf16[1024,1152]{1,0:T(8,128)(2,1)}), bf16[128,1152]{1,0:T(8,128)(2,1)}) %reduce-scatter.7.cloned.1.call-update) | async-done | bytes 294928
  362.2 6.3 collective-permute-done
  368.7 33.4 %all_gather.20 = bf16[64,2,2048]{2,0,1:T(8,128)(2,1)S(1)} all-gather(bf16[64,2,128]{2,0,1:T(8,128)(2,1)S(1)} %slice.93), channel_id=1, replica_groups=mesh['section'=8,'tensor'=16,'dp'=4] {'tensor'}, dimensions={2}, use_global_device_ids=true | all-gather | bytes 557056 | tf_op jit(solution)/shard_map/all_gather | solution.py:144
  407.5 15.1 %collective-permute-done.1 = bf16[2,8,64,256]{3,2,1,0:T(8,128)(2,1)S(1)} collective-permute-done((bf16[2,8,64,256]{3,2,1,0:T(8,128)(2,1)S(1)}, bf16[2,8,64,256]{3,2,1,0:T(8,128)(2,1)S(1)}, u32[]{:S(2)}, u32[]{:S(2)}) %collective-permute-start.1) | collective-permute-done | bytes 524320 | tf_op jit(solution)/shard_map/ppermute | solution.py:14
  424.7 15.2 %collective-permute-done.2 = bf16[2,8,64,256]{3,2,1,0:T(8,128)(2,1)S(1)} collective-permute-done((bf16[2,8,64,256]{3,2,1,0:T(8,128)(2,1)S(1)}, bf16[2,8,64,256]{3,2,1,0:T(8,128)(2,1)S(1)}, u32[]{:S(2)}, u32[]{:S(2)}) %collective-permute-start.2) | collective-permute-done | bytes 524320 | tf_op jit(solution)/shard_map/ppermute | solution.py:14
  443.6 9.1 %all-to-all-start.5 = ((bf16[16,1,64]{2,1,0:T(2,128)(2,1)}), bf16[16,1,64]{2,1,0:T(2,128)(2,1)S(1)}, u32[]{:S(2)}, u32[]{:S(2)}) async-start(bf16[16,1,64]{2,1,0:T(2,128)(2,1)} %copy.196), calls=%async_computation.5 | async-start | bytes 16384 | tf_op jit(solution)/shard_map/all_to_all | solution.py:87
  455.1 10.2 %all-to-all-done.5 = bf16[16,1,64]{2,1,0:T(2,128)(2,1)S(1)} async-done(((bf16[16,1,64]{2,1,0:T(2,128)(2,1)}), bf16[16,1,64]{2,1,0:T(2,128)(2,1)S(1)}, u32[]{:S(2)}, u32[]{:S(2)}) %all-to-all-start.5) | async-done | bytes 2080 | tf_op jit(solution)/shard_map/all_to_all | solution.py:87
  465.3 4.4 all-to-all-start.6
  473.0 14.1 %collective-permute-done.4 = bf16[2,8,64,256]{3,2,1,0:T(8,128)(2,1)S(1)} collective-permute-done((bf16[2,8,64,256]{3,2,1,0:T(8,128)(2,1)S(1)}, bf16[2,8,64,256]{3,2,1,0:T(8,128)(2,1)S(1)}, u32[]{:S(2)}, u32[]{:S(2)}) %collective-permute-start.4) | collective-permute-done | bytes 524320 | tf_op jit(solution)/shard_map/ppermute | solution.py:14
  489.3 13.1 %collective-permute-done.5 = bf16[2,8,64,256]{3,2,1,0:T(8,128)(2,1)S(1)} collective-permute-done((bf16[2,8,64,256]{3,2,1,0:T(8,128)(2,1)S(1)}, bf16[2,8,64,256]{3,2,1,0:T(8,128)(2,1)S(1)}, u32[]{:S(2)}, u32[]{:S(2)}) %collective-permute-start.5) | collective-permute-done | bytes 524320 | tf_op jit(solution)/shard_map/ppermute | solution.py:14
  508.1 10.3 %collective-permute-done.6 = bf16[2,8,64,256]{3,2,1,0:T(8,128)(2,1)} collective-permute-done((bf16[2,8,64,256]{3,2,1,0:T(8,128)(2,1)}, bf16[2,8,64,256]{3,2,1,0:T(8,128)(2,1)}, u32[]{:S(2)}, u32[]{:S(2)}) %collective-permute-start.6) | collective-permute-done | bytes 524320 | tf_op jit(solution)/shard_map/ppermute | solution.py:14
  524.5 18.4 %collective-permute-done.7 = bf16[2,8,64,256]{3,2,1,0:T(8,128)(2,1)S(1)} collective-permute-done((bf16[2,8,64,256]{3,2,1,0:T(8,128)(2,1)S(1)}, bf16[2,8,64,256]{3,2,1,0:T(8,128)(2,1)S(1)}, u32[]{:S(2)}, u32[]{:S(2)}) %collective-permute-start.7) | collective-permute-done | bytes 524320 | tf_op jit(solution)/shard_map/ppermute | solution.py:14
  544.5 28.7 %psum.14 = f32[64,2,4]{0,2,1:T(4,128)S(1)} all-reduce(f32[64,2,4]{0,2,1:T(4,128)S(1)} %fusion.84), channel_id=1, replica_groups=mesh['section'=8,'tensor'=16,'dp'=4] {'tensor'}, use_global_device_ids=true, to_apply=%region_6.7 | all-reduce | flops 512 | bytes 4096 | tf_op jit(solution)/shard_map/psum | solution.py:186
  576.5 54.0 %all-gather.9.cloned.1.call-done = bf16[512,2,512]{2,0,1:T(8,128)(2,1)} async-done(((bf16[64,2,512]{2,0,1:T(8,128)(2,1)}), bf16[512,2,512]{2,0,1:T(8,128)(2,1)}) %all-gather.9.cloned.1.call-update) | async-done | bytes 1048592 | tf_op jit(solution)/shard_map/all_gather | solution.py:195
  630.5 3.8 convolution_convert_fusion.1
  635.1 143.9 %all-reduce.2.cloned.1.call-done = bf16[512,2,1024]{2,0,1:T(8,128)(2,1)} async-done(((bf16[512,2,1024]{2,0,1:T(8,128)(2,1)}), bf16[512,2,1024]{2,0,1:T(8,128)(2,1)}) %all-reduce.2.cloned.1.call-update) | async-done | bytes 2097168 | tf_op jit(solution)/shard_map/psum | solution.py:202
  781.6 3.5 copy.202
  (149 shorter events, 68.2 us)
Async XLA Ops:
  7.2 17.9 %copy-start = (bf16[256,8,128]{2,1,0:T(8,128)(2,1)S(1)}, bf16[256,8,128]{2,1,0:T(8,128)(2,1)}, u32[]{:S(2)}) copy-start(bf16[256,8,128]{2,1,0:T(8,128)(2,1)} %param.16) | copy-start | bytes 1572868
  9.9 27.6 %all-to-all-start = ((bf16[16,1,8]{2,1,0:T(2,128)(2,1)}), bf16[16,1,8]{2,1,0:T(2,128)(2,1)S(1)}, u32[]{:S(2)}, u32[]{:S(2)}) async-start(bf16[16,1,8]{2,1,0:T(2,128)(2,1)} %copy.167), calls=%async_computation | async-start | bytes 16384 | tf_op jit(solution)/shard_map/all_to_all | solution.py:81
  25.6 15.5 %copy-start.5 = (bf16[32,2,1024]{2,1,0:T(2,128)(2,1)S(1)}, bf16[32,2,1024]{2,1,0:T(2,128)(2,1)}, u32[]{:S(2)}) copy-start(bf16[32,2,1024]{2,1,0:T(2,128)(2,1)} %param.13) | copy-start | bytes 393220
  26.9 71.0 %copy-start.9 = (bf16[256,8]{0,1:T(8,128)(2,1)S(1)}, bf16[256,8]{0,1:T(8,128)(2,1)}, u32[]{:S(2)}) copy-start(bf16[256,8]{0,1:T(8,128)(2,1)} %param.17) | copy-start | bytes 12292
  37.4 58.9 %all-to-all-start.2 = ((bf16[16,1,256,128]{3,2,1,0:T(8,128)(2,1)}), bf16[16,1,256,128]{3,2,1,0:T(8,128)(2,1)S(1)}, u32[]{:S(2)}, u32[]{:S(2)}) async-start(bf16[16,1,256,128]{3,2,1,0:T(8,128)(2,1)} %copy.172), calls=%async_computation.2 | async-start | bytes 2097152 | tf_op jit(solution)/shard_map/all_to_all | solution.py:82
  41.1 93.8 %all-gather.5.cloned.1.call-start = ((), (), s32[]{:S(2)}) async-start(), calls=%async_computation.9 | async-start | bytes 2228224 | tf_op jit(solution)/shard_map/all_gather | solution.py:108
  41.9 127.9 %all-gather.7.cloned.1.call-start = ((), (), s32[]{:S(2)}) async-start(), calls=%async_computation.10 | async-start | bytes 2621440 | tf_op jit(solution)/shard_map/all_gather | solution.py:103
  97.8 163.2 %reduce-scatter.9.cloned.1.call-start = ((), (), s32[]{:S(2)}) async-start(), calls=%async_computation.15 | async-start | bytes 294912
  144.2 211.6 %reduce-scatter.7.cloned.1.call-start = ((), (), s32[]{:S(2)}) async-start(), calls=%async_computation.14 | async-start | bytes 2654208
  169.8 2.3 copy-start.7
  180.3 13.9 %copy-start.8 = (bf16[8,4,64]{2,1,0:T(4,128)(2,1)S(1)}, bf16[8,4,64]{2,1,0:T(4,128)(2,1)}, u32[]{:S(2)}) copy-start(bf16[8,4,64]{2,1,0:T(4,128)(2,1)} %param.19) | copy-start | bytes 12292
  180.3 14.1 %copy-start.14 = (s32[128]{0:T(128)S(1)}, s32[128]{0:T(128)}, u32[]{:S(2)}) copy-start(s32[128]{0:T(128)} %param.15) | copy-start | bytes 1540
  180.3 42.3 %copy-start.6 = (bf16[4,128]{1,0:T(4,128)(2,1)S(1)}, bf16[4,128]{1,0:T(4,128)(2,1)}, u32[]{:S(2)}) copy-start(bf16[4,128]{1,0:T(4,128)(2,1)} %param.20) | copy-start | bytes 3076
  181.9 24.7 %all-to-all-start.4 = ((bf16[16,1,3]{2,1,0:T(2,128)(2,1)}), bf16[16,1,3]{2,1,0:T(2,128)(2,1)S(1)}, u32[]{:S(2)}, u32[]{:S(2)}) async-start(bf16[16,1,3]{2,1,0:T(2,128)(2,1)} %copy.186), calls=%async_computation.4 | async-start | bytes 16384 | tf_op jit(solution)/shard_map/all_to_all | solution.py:86
  206.6 15.8 %all-to-all-start.1 = ((bf16[16,2,128]{2,1,0:T(2,128)(2,1)}), bf16[16,2,128]{2,1,0:T(2,128)(2,1)S(1)}, u32[]{:S(2)}, u32[]{:S(2)}) async-start(bf16[16,2,128]{2,1,0:T(2,128)(2,1)} %reshape.326), calls=%async_computation.1 | async-start | bytes 16384 | tf_op jit(solution)/shard_map/all_to_all | solution.py:85
  359.2 9.3 %collective-permute-start = (f32[3,2,640]{2,0,1:T(4,128)S(1)}, f32[3,2,640]{2,0,1:T(4,128)S(1)}, u32[]{:S(2)}, u32[]{:S(2)}) collective-permute-start(f32[3,2,640]{2,0,1:T(4,128)S(1)} %fusion.34), channel_id=1, source_target_pairs={{0,64},{64,128},{128,192},{192,256},{256,320},{320,384},{384,448},... | collective-permute-start | bytes 46088 | tf_op jit(solution)/shard_map/ppermute | solution.py:14
  405.6 17.0 %collective-permute-start.1 = (bf16[2,8,64,256]{3,2,1,0:T(8,128)(2,1)S(1)}, bf16[2,8,64,256]{3,2,1,0:T(8,128)(2,1)S(1)}, u32[]{:S(2)}, u32[]{:S(2)}) collective-permute-start(bf16[2,8,64,256]{3,2,1,0:T(8,128)(2,1)S(1)} %get-tuple-element.35), channel_id=1, source_target_pairs={{0,64},{64,128},{128,192},{192,256},{256,320},{320,384},{384,448},... | collective-permute-start | bytes 1572872 | tf_op jit(solution)/shard_map/ppermute | solution.py:14
  422.6 20.2 %copy-start.10 = (bf16[8,64]{1,0:T(8,128)(2,1)S(1)}, bf16[8,64]{1,0:T(8,128)(2,1)}, u32[]{:S(2)}) copy-start(bf16[8,64]{1,0:T(8,128)(2,1)} %param.24) | copy-start | bytes 3076
  422.8 17.1 %collective-permute-start.2 = (bf16[2,8,64,256]{3,2,1,0:T(8,128)(2,1)S(1)}, bf16[2,8,64,256]{3,2,1,0:T(8,128)(2,1)S(1)}, u32[]{:S(2)}, u32[]{:S(2)}) collective-permute-start(bf16[2,8,64,256]{3,2,1,0:T(8,128)(2,1)S(1)} %add_convert_fusion.6), channel_id=1, source_target_pairs={{0,64},{64,128},{128,192},{192,256},{256,320},{320,384},{384,448},... | collective-permute-start | bytes 1572872 | tf_op jit(solution)/shard_map/ppermute | solution.py:14
  440.8 29.0 %collective-permute-start.3 = (bf16[2,8,64,256]{3,2,1,0:T(8,128)(2,1)}, bf16[2,8,64,256]{3,2,1,0:T(8,128)(2,1)}, u32[]{:S(2)}, u32[]{:S(2)}) collective-permute-start(bf16[2,8,64,256]{3,2,1,0:T(8,128)(2,1)} %add_convert_fusion.5), channel_id=1, source_target_pairs={{0,64},{64,128},{128,192},{192,256},{256,320},{320,384},{384,448},... | collective-permute-start | bytes 1572872 | tf_op jit(solution)/shard_map/ppermute | solution.py:14
  443.6 21.7 %all-to-all-start.5 = ((bf16[16,1,64]{2,1,0:T(2,128)(2,1)}), bf16[16,1,64]{2,1,0:T(2,128)(2,1)S(1)}, u32[]{:S(2)}, u32[]{:S(2)}) async-start(bf16[16,1,64]{2,1,0:T(2,128)(2,1)} %copy.196), calls=%async_computation.5 | async-start | bytes 16384 | tf_op jit(solution)/shard_map/all_to_all | solution.py:87
  465.3 40.1 %all-to-all-start.6 = ((bf16[16,1,64,256]{3,2,1,0:T(8,128)(2,1)}), bf16[16,1,64,256]{3,2,1,0:T(8,128)(2,1)S(1)}, u32[]{:S(2)}, u32[]{:S(2)}) async-start(bf16[16,1,64,256]{3,2,1,0:T(8,128)(2,1)} %copy.199), calls=%async_computation.6 | async-start | bytes 1048576 | tf_op jit(solution)/shard_map/all_to_all | solution.py:84
  469.8 104.9 %all-gather.11.cloned.1.call-start = ((), (), s32[]{:S(2)}) async-start(), calls=%async_computation.12 | async-start | bytes 1310720 | tf_op jit(solution)/shard_map/all_gather | solution.py:105
  471.1 16.0 %collective-permute-start.4 = (bf16[2,8,64,256]{3,2,1,0:T(8,128)(2,1)S(1)}, bf16[2,8,64,256]{3,2,1,0:T(8,128)(2,1)S(1)}, u32[]{:S(2)}, u32[]{:S(2)}) collective-permute-start(bf16[2,8,64,256]{3,2,1,0:T(8,128)(2,1)S(1)} %add_convert_fusion.4), channel_id=1, source_target_pairs={{0,64},{64,128},{128,192},{192,256},{256,320},{320,384},{384,448},... | collective-permute-start | bytes 1572872 | tf_op jit(solution)/shard_map/ppermute | solution.py:14
  487.3 15.1 %collective-permute-start.5 = (bf16[2,8,64,256]{3,2,1,0:T(8,128)(2,1)S(1)}, bf16[2,8,64,256]{3,2,1,0:T(8,128)(2,1)S(1)}, u32[]{:S(2)}, u32[]{:S(2)}) collective-permute-start(bf16[2,8,64,256]{3,2,1,0:T(8,128)(2,1)S(1)} %add_convert_fusion.3), channel_id=1, source_target_pairs={{0,64},{64,128},{128,192},{192,256},{256,320},{320,384},{384,448},... | collective-permute-start | bytes 1572872 | tf_op jit(solution)/shard_map/ppermute | solution.py:14
  503.4 15.0 %collective-permute-start.6 = (bf16[2,8,64,256]{3,2,1,0:T(8,128)(2,1)}, bf16[2,8,64,256]{3,2,1,0:T(8,128)(2,1)}, u32[]{:S(2)}, u32[]{:S(2)}) collective-permute-start(bf16[2,8,64,256]{3,2,1,0:T(8,128)(2,1)} %add_convert_fusion.2), channel_id=1, source_target_pairs={{0,64},{64,128},{128,192},{192,256},{256,320},{320,384},{384,448},... | collective-permute-start | bytes 1572872 | tf_op jit(solution)/shard_map/ppermute | solution.py:14
  506.5 123.9 %all-gather.9.cloned.1.call-start = ((), (), s32[]{:S(2)}) async-start(), calls=%async_computation.11 | async-start | bytes 1179648 | tf_op jit(solution)/shard_map/all_gather | solution.py:195
  519.6 23.3 %copy-start.3 = (f32[64,2,1024]{0,2,1:T(8,128)S(1)}, f32[64,2,1024]{0,2,1:T(8,128)}, u32[]{:S(2)}) copy-start(f32[64,2,1024]{0,2,1:T(8,128)} %copy-done.2) | copy-start | bytes 1572868
  519.6 23.2 %collective-permute-start.7 = (bf16[2,8,64,256]{3,2,1,0:T(8,128)(2,1)S(1)}, bf16[2,8,64,256]{3,2,1,0:T(8,128)(2,1)S(1)}, u32[]{:S(2)}, u32[]{:S(2)}) collective-permute-start(bf16[2,8,64,256]{3,2,1,0:T(8,128)(2,1)S(1)} %add_convert_fusion.1), channel_id=1, source_target_pairs={{0,64},{64,128},{128,192},{192,256},{256,320},{320,384},{384,448},... | collective-permute-start | bytes 1572872 | tf_op jit(solution)/shard_map/ppermute | solution.py:14
  574.4 204.6 %all-reduce.2.cloned.1.call-start = ((), (), s32[]{:S(2)}) async-start(), calls=%async_computation.13 | async-start | bytes 4194304 | tf_op jit(solution)/shard_map/psum | solution.py:202
  630.5 3.9 copy-start.4
  634.3 144.7 %copy-start.1 = (bf16[512,2,1024]{2,0,1:T(8,128)(2,1)S(1)}, bf16[512,2,1024]{2,0,1:T(8,128)(2,1)}, u32[]{:S(2)}) copy-start(bf16[512,2,1024]{2,0,1:T(8,128)(2,1)} %all-gather.5.cloned.1.call-done) | copy-start | bytes 6291460
  (4 other events, 3.0 us)
Sparse Core Ops, SparseCore 0:
  44.6 90.2 all-gather.4
  137.5 32.1 all-gather.6
  174.7 86.2 reduce-scatter.8
  265.5 90.3 reduce-scatter.6
  506.7 29.0 all-gather.10
  574.5 55.9 all-gather.8
  634.5 144.4 all-reduce.1
where the time goes:
time: 793 us; the launch traced here: 792 us
  waiting for transfers between devices  557 us (70%)
  blocking collectives  87.1 us (11%)
  starting transfers between devices  65.2 us (8%)
  local copies, waits for them, and re-layouts  36.1 us (5%)
  matrix products  22.4 us (3%)
  between operations  14.7 us (2%)
  other arithmetic  9.71 us (1%)
    psum x1, waiting for transfers between devices, per_device(): lax.psum(partial_sum.astype(jnp.bfloat16), 'tensor').astype(jnp.float32)  144 us
    unnamed x9, waiting for transfers between devices  132 us
    ppermute x8, waiting for transfers between devices, passed_along(): return lax.ppermute(value, axis, pairs)  92.4 us
    all_to_all x1, waiting for transfers between devices, per_device(): lax.all_to_all(sending[1], 'tensor', split_axis=0, concat_axis=0, tiled=T...  54.3 us
    all_gather x1, waiting for transfers between devices, per_device(): piece = lax.all_gather(normed, 'section', axis=0, tiled=True)  54 us
    all_gather x1, blocking collectives, per_device(): lax.all_gather(convolved[..., inner:], 'tensor', axis=2, tiled=True)  33.4 us
    psum x1, blocking collectives, per_device(): group_squares = lax.psum(group_squares, 'tensor')  28.7 us
    all_gather x1, waiting for transfers between devices, per_device(): lax.all_gather(new_xz, 'dp', axis=0, tiled=True)  25.5 us
  transfers between devices with their start and end apart: 21, of which 18 were waited for; matrix products, arithmetic and copies ran while one was open for 6% of the time, Pallas kernels for 0%

commit v1 on v0

v1 whole, which is shorter than its diff:
```python
import jax
import jax.numpy as jnp
from jax import lax
from jax.experimental import pallas as pl
from jax.experimental.pallas import tpu as pltpu
from jax.sharding import PartitionSpec as P

STATE = 256
GROUP_HEADS = 32
KERNEL = 4
MESH = pl.DeviceIdType.MESH
NZ, NS, ND = 16, 8, 4
VMEM = pl.BlockSpec(memory_space=pltpu.VMEM)
SMEM = pl.BlockSpec(memory_space=pltpu.SMEM)
F32, BF16 = jnp.float32, jnp.bfloat16
ARRIVAL = (0, -1, 1, -2, 2, -3, 3, -4, 4, -5, 5, -6, 6, -7, 7, -8)


def place():
    return lax.axis_index("section"), lax.axis_index("tensor"), lax.axis_index("dp")


def turn(index, by, size):
    return lax.rem(index + (by % size), size)


def greet(peers):
    barrier = pltpu.get_barrier_semaphore()
    for peer in peers:
        pl.semaphore_signal(barrier, inc=1, device_id=peer, device_id_type=MESH)
    pl.semaphore_wait(barrier, len(peers))


def send(source, target, send_sem, recv_sem, peer):
    copy = pltpu.make_async_remote_copy(
        src_ref=source,
        dst_ref=target,
        send_sem=send_sem,
        recv_sem=recv_sem,
        device_id=peer,
        device_id_type=MESH,
    )
    copy.start()
    return copy


def dims(lhs, rhs):
    return (((lhs,), (rhs,)), ((), ()))


def project_kernel(
    groups_ref, act_ref, xz_ref, dt_ref, bc_ref, out_ref, taps_ref,
    heads_out, steps_out, bc_out, rows_out,
    acts, weights, dts, parts, parts_in, bc_parts, bc_in, step_parts, steps_in,
    bc_all, chosen,
    w_send, w_recv, d_send, d_recv, o_send, o_recv, right_send, right_recv,
    left_send, left_recv, p_send, p_recv, b_send, b_recv, s_send, s_recv,
    z_send, z_recv, c_send, c_recv,
):
    s, t, d = place()
    right, left = (s, turn(t, 1, NZ), d), (s, turn(t, -1, NZ), d)
    sections = [turn(s, k, NS) for k in range(1, NS)]
    core = d + 1 - 2 * lax.rem(d, 2)
    across = turn(d, 2, ND)
    greet(
        [(s, turn(t, k, NZ), d) for k in range(1, NZ)]
        + [(p, t, d) for p in sections]
        + [(s, t, core), (s, t, across)]
    )
    sent = []

    def rows_at(index):
        return weights.at[pl.ds(pl.multiple_of(index * 256, 256), 256)]

    gathers = []
    for own, slot_of, ss, rs in (
        (xz_ref, rows_at, w_send, w_recv),
        (dt_ref, lambda i: dts.at[i], d_send, d_recv),
        (out_ref, lambda i: rows_out.at[i], o_send, o_recv),
    ):
        near = send(own, slot_of(d), ss.at[0], rs.at[0], (s, t, core))
        far = send(own, slot_of(d), ss.at[1], rs.at[1], (s, t, across))
        sent += [near, far]
        gathers.append((slot_of, ss, rs, near, far))

    def start_ring(c):
        rows = pl.ds(32 * c, 32)
        return [
            send(act_ref.at[rows], acts.at[t, rows], right_send.at[0, c], right_recv.at[0, c], right),
            send(act_ref.at[rows], acts.at[t, rows], left_send.at[0, c], left_recv.at[0, c], left),
        ]

    rings = [start_ring(0), start_ring(1)]
    sent += rings[0] + rings[1]
    acts[t] = act_ref[...]
    weights[pl.ds(pl.multiple_of(d * 256, 256), 256), :] = xz_ref[...]
    dts[d] = dt_ref[...]
    rows_out[d] = out_ref[...]

    forwarded = []

    def forward_weights():
        for slot_of, ss, rs, near, far in gathers:
            far.wait_recv()
            copy = send(slot_of(across), slot_of(across), ss.at[2], rs.at[2], (s, t, core))
            forwarded.append(copy)
            sent.append(copy)

    def have_weights():
        for (slot_of, ss, rs, near, far), copy in zip(gathers[:2], forwarded[:2]):
            near.wait_recv()
            copy.wait_recv()

    def block_of(i):
        return turn(t, ARRIVAL[i], NZ)

    part_copies = []

    def project(group):
        rows = jnp.concatenate([acts[block_of(4 * group + i)] for i in range(4)], axis=0)
        for half in range(2):
            product = jnp.dot(
                rows, weights[:, 512 * half : 512 * half + 512], preferred_element_type=F32
            ).astype(BF16)
            for j in range(4):
                parts[4 * half + j, 4 * group : 4 * group + 4] = product[
                    :, 128 * j : 128 * j + 128
                ].reshape(4, 64, 128)
        for k in range(1, NS):
            span = pl.ds(4 * group, 4)
            copy = send(
                parts.at[sections[k - 1], span],
                parts_in.at[k - 1, span],
                p_send.at[k - 1, group],
                p_recv.at[k - 1, group],
                (sections[k - 1], t, d),
            )
            part_copies.append(copy)
            sent.append(copy)

    for step in range(1, 9):
        for c in range(2):
            rows = pl.ds(32 * c, 32)
            rings[c][0].wait_recv()
            if step < 8:
                block = turn(t, -step, NZ)
                copy = send(
                    acts.at[block, rows], acts.at[block, rows],
                    right_send.at[step, c], right_recv.at[step, c], right,
                )
                rings[c][0] = copy
                sent.append(copy)
            if step < 8:
                rings[c][1].wait_recv()
            if step < 7:
                block = turn(t, step, NZ)
                copy = send(
                    acts.at[block, rows], acts.at[block, rows],
                    left_send.at[step, c], left_recv.at[step, c], left,
                )
                rings[c][1] = copy
                sent.append(copy)
        if step == 3:
            forward_weights()
        if step == 4:
            have_weights()
            project(0)
        if step == 5:
            project(1)
        if step == 6:
            project(2)

    bc_parts[0] = jnp.zeros((64, 128), BF16)
    for i in range(4):
        product = jnp.dot(
            acts[4 * i : 4 * i + 4].reshape(256, 1024), bc_ref[...], preferred_element_type=F32
        )
        bc_parts[1 + 4 * i : 5 + 4 * i] = product.astype(BF16).reshape(4, 64, 128)
    bc_copies = []
    for k in range(1, NS):
        copy = send(
            bc_parts.at[pl.ds(2 * sections[k - 1], 3)],
            bc_in.at[k - 1],
            b_send.at[k - 1],
            b_recv.at[k - 1],
            (sections[k - 1], t, d),
        )
        bc_copies.append(copy)
        sent.append(copy)
    project(3)
    raw = jnp.zeros((16, 1024), F32)
    for i in range(ND):
        raw = raw + lax.dot_general(
            dts[i],
            acts[:, :, 256 * i : 256 * i + 256].reshape(1024, 256),
            dims(1, 1),
            preferred_element_type=F32,
        )
    for j in range(NS):
        for r in range(8):
            step_parts[j, r : r + 1, :] = raw[j : j + 1, 128 * r : 128 * r + 128]
    step_copies = []
    for k in range(1, NS):
        copy = send(
            step_parts.at[sections[k - 1]],
            steps_in.at[k - 1],
            s_send.at[k - 1],
            s_recv.at[k - 1],
            (sections[k - 1], t, d),
        )
        step_copies.append(copy)
        sent.append(copy)

    for copy in bc_copies:
        copy.wait_recv()
    total = bc_parts[pl.ds(2 * s, 3)].astype(F32)
    for k in range(NS - 1):
        total = total + bc_in[k].astype(F32)
    for m in range(2):
        rows = total[:, 32 * m : 32 * m + 32, :].reshape(96, 128)
        u = jnp.zeros((64, 128), F32)
        for k in range(KERNEL):
            u = u + taps_ref[k : k + 1, :] * rows[29 + k : 93 + k]
        u = (u / (1.0 + jnp.exp(-u))).astype(BF16)
        bc_all[t, 32 * m : 32 * m + 32, :] = u[:32]
        bc_all[t, 64 + 32 * m : 96 + 32 * m, :] = u[32:]
    z_copies = []
    for k in range(1, NZ):
        copy = send(
            bc_all.at[t], bc_all.at[t], z_send.at[k - 1], z_recv.at[k - 1], (s, turn(t, k, NZ), d)
        )
        z_copies.append(copy)
        sent.append(copy)
    for copy in z_copies:
        copy.wait_recv()

    def choose(section, j):
        return bc_all[8 * (j // 2) + 2 * groups_ref[section] + j % 2]

    choice_copies = []
    for k in range(1, NS):
        for j in range(4):
            chosen[k - 1, j] = choose(sections[k - 1], j)
        copy = send(
            chosen.at[k - 1], bc_out.at[s], c_send.at[k - 1], c_recv.at[k - 1],
            (sections[k - 1], t, d),
        )
        choice_copies.append(copy)
        sent.append(copy)
    for j in range(4):
        bc_out[s, j] = choose(s, j)

    for copy in part_copies + step_copies:
        copy.wait_recv()
    for i in range(NZ):
        value = parts[s, i].astype(F32)
        for k in range(NS - 1):
            value = value + parts_in[k, i].astype(F32)
        heads_out[block_of(i)] = value
    value = step_parts[s]
    for k in range(NS - 1):
        value = value + steps_in[k]
    steps_out[...] = value

    gathers[2][3].wait_recv()
    forwarded[2].wait_recv()
    for copy in choice_copies:
        copy.wait_recv()
    for copy in sent:
        copy.wait_send()


def project_call(groups, act, xz, dt, bc, out, taps):
    dma = pltpu.SemaphoreType.DMA
    return pl.pallas_call(
        project_kernel,
        out_shape=(
            jax.ShapeDtypeStruct((NZ, 64, 128), F32),
            jax.ShapeDtypeStruct((8, 128), F32),
            jax.ShapeDtypeStruct((NS, 4, 128, 128), BF16),
            jax.ShapeDtypeStruct((ND, 512, 256), BF16),
        ),
        in_specs=[SMEM] + [VMEM] * 6,
        out_specs=(VMEM,) * 4,
        scratch_shapes=[
            pltpu.VMEM((NZ, 64, 1024), BF16),
            pltpu.VMEM((1024, 1024), BF16),
            pltpu.VMEM((ND, 16, 256), BF16),
            pltpu.VMEM((NS, NZ, 64, 128), BF16),
            pltpu.VMEM((NS - 1, NZ, 64, 128), BF16),
            pltpu.VMEM((NZ + 1, 64, 128), BF16),
            pltpu.VMEM((NS - 1, 3, 64, 128), BF16),
            pltpu.VMEM((NS, 8, 128), F32),
            pltpu.VMEM((NS - 1, 8, 128), F32),
            pltpu.VMEM((NZ, 128, 128), BF16),
            pltpu.VMEM((NS - 1, 4, 128, 128), BF16),
            dma((3,)), dma((3,)), dma((3,)), dma((3,)), dma((3,)), dma((3,)),
            dma((8, 2)), dma((8, 2)), dma((8, 2)), dma((8, 2)),
            dma((NS - 1, 4)), dma((NS - 1, 4)),
            dma((NS - 1,)), dma((NS - 1,)), dma((NS - 1,)), dma((NS - 1,)),
            dma((NZ - 1,)), dma((NZ - 1,)), dma((NS - 1,)), dma((NS - 1,)),
        ],
        compiler_params=pltpu.CompilerParams(
            collective_id=0, has_side_effects=True, vmem_limit_bytes=40 << 20
        ),
        cost_estimate=pl.CostEstimate(
            flops=3_000_000_000, bytes_accessed=100_000_000, transcendentals=0
        ),
    )(groups, act, xz, dt, bc, out, taps)


def scan_kernel(heads_ref, step_ref, log_ref, bc_ref, taps_ref, gated_out):
    lane = lax.broadcasted_iota(jnp.int32, (128, 128), 1)
    row = lax.broadcasted_iota(jnp.int32, (128, 128), 0)
    causal = row >= lane
    upto = (row <= lane).astype(F32)
    same = (row == lane).astype(F32)
    exact = lax.Precision.HIGHEST
    cum = jnp.dot(log_ref[...], upto, precision=exact, preferred_element_type=F32)
    step = step_ref[...]
    both = jnp.concatenate([cum, step], axis=0)
    columns = lax.dot_general(same, both, dims(1, 1), precision=exact, preferred_element_type=F32)
    tall = lax.broadcasted_iota(jnp.int32, (512, 128), 0)
    gated = []
    for m in range(2):
        v = heads_ref[:, 32 * m : 32 * m + 32, :].reshape(512, 128)
        u = taps_ref[3:4, :] * v
        for back in range(1, KERNEL):
            moved = jnp.where(tall >= back, pltpu.roll(v, back, 0), 0.0)
            u = u + taps_ref[3 - back : 4 - back, :] * moved
        x = (u / (1.0 + jnp.exp(-u))).astype(BF16)
        state = jnp.zeros((STATE, 128), F32)
        outs = []
        for c in range(4):
            at = 4 * m + c

            def pick(j):
                part = bc_ref[2 * c : 2 * c + 2, j].reshape(2, 2, 2, 32, 128)
                return part[:, :, m].reshape(128, 128)

            b = jnp.concatenate([pick(0), pick(1)], axis=1)
            cc = jnp.concatenate([pick(2), pick(3)], axis=1)
            xc = x[128 * c : 128 * c + 128]
            xf = xc.astype(F32)
            cum_c, step_c = columns[:, at : at + 1], columns[:, 8 + at : 9 + at]
            cum_r, step_r = cum[at : at + 1, :], step[at : at + 1, :]
            scores = lax.dot_general(cc, b, dims(1, 1), preferred_element_type=F32)
            mixing = jnp.exp(jnp.where(causal, cum_c - cum_r, -1e30)) * step_r
            y = jnp.dot((scores * mixing).astype(BF16), xc, preferred_element_type=F32)
            y = y + jnp.exp(cum_c) * jnp.dot(cc, state.astype(BF16), preferred_element_type=F32)
            y = y + taps_ref[4:5, :] * xf
            outs.append(y)
            if c < 3:
                end = cum[at : at + 1, 127:128]
                tail = (jnp.exp(end - cum_c) * step_c * xf).astype(BF16)
                state = jnp.exp(end) * state + lax.dot_general(
                    b, tail, dims(0, 0), preferred_element_type=F32
                )
        z = pltpu.roll(v, 64, 1)
        gated.append(jnp.concatenate(outs, axis=0) * (z / (1.0 + jnp.exp(-z))))
    wide = lax.broadcasted_iota(jnp.int32, (512, 128), 1)
    gated_out[...] = jnp.where(wide < 64, gated[0], pltpu.roll(gated[1], 64, 1)).astype(BF16)


def scan_call(heads, step, log_decay, bc, taps):
    return pl.pallas_call(
        scan_kernel,
        out_shape=jax.ShapeDtypeStruct((512, 128), BF16),
        in_specs=[VMEM] * 5,
        out_specs=VMEM,
        compiler_params=pltpu.CompilerParams(vmem_limit_bytes=32 << 20),
        cost_estimate=pl.CostEstimate(
            flops=200_000_000, bytes_accessed=3_000_000, transcendentals=500_000
        ),
    )(heads, step, log_decay, bc, taps)


def mix_kernel(
    gated_ref, rows_ref, act_ref, hot_ref, gain_ref,
    mixed_out,
    gathered, squares, squares_in, totals, product, right_out, right_in, left_out, left_in,
    g_send, g_recv, q_send, q_recv, y_send, y_recv,
    right_send, right_recv, left_send, left_recv,
    gr_send, gr_recv, gl_send, gl_recv,
):
    s, t, d = place()
    right, left = (s, turn(t, 1, NZ), d), (s, turn(t, -1, NZ), d)
    sections = [turn(s, k, NS) for k in range(1, NS)]
    y = lax.rem(s, 4)
    columns = [s - y + turn(y, k, 4) for k in range(1, 4)]
    greet([(s, turn(t, k, NZ), d) for k in range(1, NZ)] + [(p, t, d) for p in sections])
    sent = []

    copies = []
    for k in range(1, NS):
        copy = send(
            gated_ref, gathered.at[s], g_send.at[k - 1], g_recv.at[k - 1], (sections[k - 1], t, d)
        )
        copies.append(copy)
    gathered[s] = gated_ref[...]
    sent += copies
    for copy in copies:
        copy.wait_recv()

    for j in range(4):
        value = jnp.zeros((8, 128), F32)
        for i in range(NS):
            part = gathered[i, 128 * j : 128 * j + 128, :].astype(F32)
            value = value + lax.dot_general(
                hot_ref[:8, 128 * i : 128 * i + 128],
                (part * part).astype(BF16),
                dims(1, 1),
                preferred_element_type=F32,
            )
        squares[j] = value
    copies = []
    for k in range(1, NZ):
        copy = send(
            squares.at[y], squares_in.at[k - 1], q_send.at[k - 1], q_recv.at[k - 1],
            (s, turn(t, k, NZ), d),
        )
        copies.append(copy)
    sent += copies
    for copy in copies:
        copy.wait_recv()
    value = squares[y]
    for k in range(NZ - 1):
        value = value + squares_in[k]
    totals[y] = value
    copies = []
    for k in range(3):
        copy = send(
            totals.at[y], totals.at[y], y_send.at[k], y_recv.at[k], (columns[k], t, d)
        )
        copies.append(copy)
    sent += copies
    for copy in copies:
        copy.wait_recv()

    wide = lax.broadcasted_iota(jnp.int32, (128, 128), 1)
    for j in range(4):
        inverse = lax.rsqrt(totals[j] / (GROUP_HEADS * 64) + 1e-05)
        high = inverse.astype(BF16)
        low = (inverse - high.astype(F32)).astype(BF16)
        scale = lax.dot_general(
            jnp.concatenate([high, low], axis=0), hot_ref[...], dims(0, 0),
            preferred_element_type=F32,
        )
        first, second = [], []
        for i in range(0, NS, 2):
            pair = []
            for h in (i, i + 1):
                span = slice(128 * h, 128 * h + 128)
                value = gathered[h, 128 * j : 128 * j + 128, :].astype(F32)
                pair.append(value * scale[:, span] * gain_ref[0:1, span])
            even, odd = pair
            first.append(jnp.where(wide < 64, even, pltpu.roll(odd, 64, 1)).astype(BF16))
            second.append(jnp.where(wide < 64, pltpu.roll(even, 64, 1), odd).astype(BF16))
        lhs = jnp.concatenate(
            [jnp.concatenate(first, axis=1), jnp.concatenate(second, axis=1)], axis=0
        )
        for i in range(ND):
            result = jnp.dot(lhs, rows_ref[i], preferred_element_type=F32)
            for m in range(2):
                product[
                    4 * j : 4 * j + 4, 32 * m : 32 * m + 32, 256 * i : 256 * i + 256
                ] = result[128 * m : 128 * m + 128].reshape(4, 32, 256)

    from_left, from_right = [None, None], [None, None]
    for step in range(8):
        for h in range(2):
            span = slice(512 * h, 512 * h + 512)
            value = product[turn(t, 8 - step, NZ), :, span]
            if step > 0:
                from_left[h].wait_recv()
                value = value + right_in[step - 1, h].astype(F32)
            right_out[step, h] = value.astype(BF16)
            from_left[h] = send(
                right_out.at[step, h], right_in.at[step, h],
                right_send.at[step, h], right_recv.at[step, h], right,
            )
            sent.append(from_left[h])
            if step < 7:
                value = product[turn(t, step - 7, NZ), :, span]
                if step > 0:
                    from_right[h].wait_recv()
                    value = value + left_in[step - 1, h].astype(F32)
                left_out[step, h] = value.astype(BF16)
                from_right[h] = send(
                    left_out.at[step, h], left_in.at[step, h],
                    left_send.at[step, h], left_recv.at[step, h], left,
                )
                sent.append(from_right[h])
    for h in range(2):
        span = slice(512 * h, 512 * h + 512)
        from_left[h].wait_recv()
        from_right[h].wait_recv()
        value = product[t, :, span] + act_ref[:, span].astype(F32)
        value = value + right_in[7, h].astype(F32) + left_in[6, h].astype(F32)
        mixed_out[t, :, span] = value.astype(BF16)

    rings = [[None, None], [None, None]]
    for step in range(9):
        for c in range(2):
            rows = pl.ds(32 * c, 32)
            if step > 0:
                rings[c][0].wait_recv()
            if step < 8:
                block = turn(t, -step, NZ)
                rings[c][0] = send(
                    mixed_out.at[block, rows], mixed_out.at[block, rows],
                    gr_send.at[step, c], gr_recv.at[step, c], right,
                )
                sent.append(rings[c][0])
            if 0 < step < 8:
                rings[c][1].wait_recv()
            if step < 7:
                block = turn(t, step, NZ)
                rings[c][1] = send(
                    mixed_out.at[block, rows], mixed_out.at[block, rows],
                    gl_send.at[step, c], gl_recv.at[step, c], left,
                )
                sent.append(rings[c][1])
    for copy in sent:
        copy.wait_send()


def mix_call(gated, rows, act, hot, gain):
    dma = pltpu.SemaphoreType.DMA
    return pl.pallas_call(
        mix_kernel,
        out_shape=jax.ShapeDtypeStruct((NZ, 64, 1024), BF16),
        in_specs=[VMEM] * 5,
        out_specs=VMEM,
        scratch_shapes=[
            pltpu.VMEM((NS, 512, 128), BF16),
            pltpu.VMEM((4, 8, 128), F32),
            pltpu.VMEM((NZ - 1, 8, 128), F32),
            pltpu.VMEM((4, 8, 128), F32),
            pltpu.VMEM((NZ, 64, 1024), F32),
            pltpu.VMEM((8, 2, 64, 512), BF16),
            pltpu.VMEM((8, 2, 64, 512), BF16),
            pltpu.VMEM((7, 2, 64, 512), BF16),
            pltpu.VMEM((7, 2, 64, 512), BF16),
            dma((NS - 1,)), dma((NS - 1,)), dma((NZ - 1,)), dma((NZ - 1,)), dma((3,)), dma((3,)),
            dma((8, 2)), dma((8, 2)), dma((7, 2)), dma((7, 2)),
            dma((8, 2)), dma((8, 2)), dma((7, 2)), dma((7, 2)),
        ],
        compiler_params=pltpu.CompilerParams(
            collective_id=1, has_side_effects=True, vmem_limit_bytes=40 << 20
        ),
        cost_estimate=pl.CostEstimate(
            flops=1_100_000_000, bytes_accessed=100_000_000, transcendentals=0
        ),
    )(gated, rows, act, hot, gain)


def relay(old_heads, new_heads, xz_weight, out_weight):
    owners = lax.axis_size("tensor")
    member = lax.axis_index("tensor")
    head_dev = xz_weight.shape[1]
    mine_old = lax.dynamic_slice_in_dim(old_heads, member * head_dev, head_dev)
    mine_new = lax.dynamic_slice_in_dim(new_heads, member * head_dev, head_dev)
    numbers = jnp.arange(old_heads.shape[0], dtype=jnp.int32)
    position = jnp.sum(
        jnp.where(new_heads[None, :] == mine_old[:, None], numbers[None, :], 0), axis=1
    )
    origin = jnp.sum(
        jnp.where(old_heads[None, :] == mine_new[:, None], numbers[None, :], 0), axis=1
    )
    devices = jnp.arange(owners, dtype=jnp.int32)
    chosen = (position[None, :] // head_dev == devices[:, None]).astype(BF16)
    placing = (origin[None, :] // head_dev == devices[:, None]).astype(BF16)

    def select(form, mask, array):
        return jnp.einsum(form, mask, array, preferred_element_type=F32).astype(BF16)

    def exchange(array):
        return lax.all_to_all(array, "tensor", split_axis=0, concat_axis=0, tiled=True)

    moved_xz = exchange(select("dj,rjq->drq", chosen, xz_weight))
    moved_out = exchange(select("dj,jer->der", chosen, out_weight))
    new_xz = select("sk,srq->rkq", placing, moved_xz)
    new_out = select("sk,ser->ker", placing, moved_out)
    return new_xz, new_out


def per_device(
    activations,
    old_heads,
    new_heads,
    xz_weight,
    dt_weight,
    bc_weight,
    conv_heads,
    conv_groups,
    decay_log,
    dt_bias,
    skip_gain,
    norm_gain,
    out_weight,
):
    s, t, _ = place()
    head_dev = xz_weight.shape[1]
    groups = lax.dynamic_slice_in_dim(old_heads, t * head_dev, head_dev) // GROUP_HEADS
    act = jnp.transpose(activations, (1, 0, 2)).reshape(64, 1024)
    step_rows = jnp.pad(jnp.transpose(dt_weight), ((0, 8), (0, 0)))
    heads, raw, bc, rows = project_call(
        groups,
        act,
        xz_weight.reshape(256, 1024),
        step_rows,
        bc_weight,
        out_weight.reshape(512, 256),
        jnp.pad(conv_groups.astype(F32), ((0, 4), (0, 0))),
    )

    def own(array):
        return lax.dynamic_index_in_dim(array, s, 0, keepdims=False).astype(F32)

    raw = jnp.transpose(raw.reshape(4, 4, 2, 32), (2, 0, 1, 3)).reshape(8, 128)
    step = jax.nn.softplus(raw + own(dt_bias))
    log_decay = -step * jnp.exp(own(decay_log))
    taps = own(conv_heads)
    taps = jnp.concatenate([taps, taps], axis=1)
    skip = jnp.broadcast_to(own(skip_gain), (4, 128))
    gated = scan_call(heads, step, log_decay, bc, jnp.concatenate([taps, skip], axis=0))

    index = jnp.arange(8, dtype=jnp.int32)
    hot = (
        (index[:, None, None] % 4 == groups[None, :, None])
        & (index[:, None, None] // 4 == jnp.arange(2, dtype=jnp.int32)[None, None, :])
    ).astype(BF16)
    hot = jnp.broadcast_to(hot[:, :, :, None], (8, 8, 2, 64)).reshape(8, 1024)
    hot = jnp.concatenate([hot, hot], axis=0)
    gain = jnp.broadcast_to(norm_gain.astype(F32)[:, None, :], (8, 2, 64)).reshape(1, 1024)
    gain = jnp.broadcast_to(gain, (8, 1024))
    mixed = mix_call(gated, rows, act, hot, gain)
    mixed = jnp.transpose(mixed.reshape(16, 2, 32, 1024), (0, 2, 1, 3)).reshape(512, 2, 1024)
    new_xz, new_out = relay(old_heads, new_heads, xz_weight, out_weight)
    return mixed, new_xz, new_out


def solution(mesh):
    in_specs = (
        P("tensor", "dp", "section"),
        P(),
        P(),
        P(("section", "dp"), "tensor", None),
        P(("section", "dp"), "tensor"),
        P("section", "tensor"),
        P("tensor", None, None),
        P(None, "tensor"),
        P("tensor"),
        P("tensor"),
        P("tensor"),
        P("tensor", None),
        P("tensor", None, ("section", "dp")),
    )
    out_specs = (
        P(None, "dp", "section"),
        P(("section", "dp"), "tensor", None),
        P("tensor", None, ("section", "dp")),
    )
    return jax.shard_map(
        per_device, mesh=mesh, in_specs=in_specs, out_specs=out_specs, check_vma=False
    )
```

time: 793 us -> 302 us (0.38)
  waiting for transfers between devices: 557 us -> 27.2 us
  Pallas kernels: 0 us -> 226 us
  blocking collectives: 87.1 us -> 0 us
  starting transfers between devices: 65.2 us -> 21.5 us
  local copies, waits for them, and re-layouts: 36.1 us -> 11.2 us
  matrix products: 22.4 us -> 5.01 us
  between operations: 14.7 us -> 2.29 us
    pallas_call x0 -> x3, Pallas kernels: none -> 226 us  [the longest x1 125 us: project_call(): pl.pallas_call(project_kernel, out_shape=(jax.ShapeDtypeStruct((NZ, 64, 1...]
    psum x1 -> x0, waiting for transfers between devices: 144 us -> none  [per_device(): lax.psum(partial_sum.astype(jnp.bfloat16), 'tensor').astype(jnp.float32)]
    unnamed x9 -> x0, waiting for transfers between devices: 132 us -> none
    ppermute x8 -> x0, waiting for transfers between devices: 92.4 us -> none  [passed_along(): return lax.ppermute(value, axis, pairs)]
    all_gather x4 -> x0, waiting for transfers between devices: 90 us -> none  [the longest x1 54 us: per_device(): piece = lax.all_gather(normed, 'section', axis=0, tiled=True)]
    all_to_all x6 -> x2, waiting for transfers between devices: 98.5 us -> 27.2 us  [exchange(): lax.all_to_all(array, 'tensor', split_axis=0, concat_axis=0, tiled=True)]
    all_gather x2 -> x0, blocking collectives: 38.6 us -> none  [the longest x1 33.4 us: per_device(): lax.all_gather(convolved[..., inner:], 'tensor', axis=2, tiled=True)]
    psum x1 -> x0, blocking collectives: 28.7 us -> none  [per_device(): group_squares = lax.psum(group_squares, 'tensor')]
  transfers between devices with their start and end apart: 21 -> 2, of which waited for: 18 -> 1; matrix products, arithmetic and copies ran while one was open for 6% -> 3% of each run, Pallas kernels for 0% -> 76%
where the time goes in v1:
time: 302 us; the launch traced here: 296 us
  Pallas kernels  226 us (75%)
  waiting for transfers between devices  27.2 us (9%)
  starting transfers between devices  21.5 us (7%)
  local copies, waits for them, and re-layouts  11.2 us (4%)
  matrix products  5.01 us (2%)
    pallas_call x1, Pallas kernels, project_call(): pl.pallas_call(project_kernel, out_shape=(jax.ShapeDtypeStruct((NZ, 64, 1...  125 us
    pallas_call x1, Pallas kernels, mix_call(): pl.pallas_call(mix_kernel, out_shape=jax.ShapeDtypeStruct((NZ, 64, 1024),...  99.5 us
    all_to_all x2, waiting for transfers between devices, exchange(): lax.all_to_all(array, 'tensor', split_axis=0, concat_axis=0, tiled=True)  27.2 us
    all_to_all x2, starting transfers between devices, exchange(): lax.all_to_all(array, 'tensor', split_axis=0, concat_axis=0, tiled=True)  21.5 us
  transfers between devices with their start and end apart: 2, of which 1 were waited for; matrix products, arithmetic and copies ran while one was open for 3% of the time, Pallas kernels for 76%

profile of v1, /device:TPU:6, one launch (start us, length us, event | category | flops | bytes accessed | tf_op | source)
XLA Modules:
  0.0 296.1 jit_solution(18350270156133141921)
XLA Ops:
  0.7 0.8 and_select_fusion.4
  1.5 0.8 select_reduce_fusion.1
  2.3 1.4 convolution_convert_fusion.2
  3.7 1.0 copy.32
  4.6 15.2 %all-to-all-start.1 = ((bf16[16,64,256]{2,1,0:T(8,128)(2,1)}), bf16[16,64,256]{2,1,0:T(8,128)(2,1)S(1)}, u32[]{:S(2)}, u32[]{:S(2)}) async-start(bf16[16,64,256]{2,1,0:T(8,128)(2,1)} %copy.32), calls=%async_computation.1 | async-start | bytes 1048576 | tf_op jit(solution)/shard_map/all_to_all | solution.py:579
  19.8 0.5 convolution_convert_fusion
  20.4 1.3 copy.29
  21.7 27.2 %all-to-all-done.1 = bf16[16,64,256]{2,1,0:T(8,128)(2,1)S(1)} async-done(((bf16[16,64,256]{2,1,0:T(8,128)(2,1)}), bf16[16,64,256]{2,1,0:T(8,128)(2,1)S(1)}, u32[]{:S(2)}, u32[]{:S(2)}) %all-to-all-start.1) | async-done | bytes 524320 | tf_op jit(solution)/shard_map/all_to_all | solution.py:579
  48.9 6.3 %all-to-all-start = ((bf16[16,256,128]{2,1,0:T(8,128)(2,1)}), bf16[16,256,128]{2,1,0:T(8,128)(2,1)}, u32[]{:S(2)}, u32[]{:S(2)}) async-start(bf16[16,256,128]{2,1,0:T(8,128)(2,1)} %copy.29), calls=%async_computation | async-start | bytes 2097152 | tf_op jit(solution)/shard_map/all_to_all | solution.py:579
  55.3 0.1 dynamic_slice.26
  55.4 0.1 copy.44
  55.5 0.6 dynamic_slice.22
  56.9 124.5 %shard_map.148 = (f32[16,64,128]{2,1,0:T(8,128)S(1)}, f32[8,128]{1,0:T(8,128)S(1)}, bf16[8,4,128,128]{3,2,1,0:T(8,128)(2,1)S(1)}, bf16[4,512,256]{2,1,0:T(8,128)(2,1)S(1)}) custom-call(s32[8]{0:T(128)S(1)} %get-tuple-element.20.groups_ref, bf16[64,1024]{1,0:T(8,128)(2,1)S(1)} %bitcast.35, bf16[256,1024]{1,0:T(8,128)(2,1)S(1)} %bitcast.33, ...), custom_call_target="tpu_custom_call" | custom-call | flops 3000000000 | bytes 100000000 | tf_op jit(solution)/shard_map/pallas_call | solution.py:275
  181.4 1.0 copy-done.3
  182.3 0.1 add.72
  182.4 0.1 add.74
  182.5 0.6 dynamic_slice.23
  183.8 0.6 dynamic_slice.25
  184.4 0.1 iota_compare_fusion.3
  184.6 0.1 and_convert_fusion
  184.6 0.1 broadcast_in_dim.22
  184.8 0.1 reshape.225
  184.9 0.1 broadcast_in_dim.28
  185.0 0.7 fusion.13.taps_ref
  185.7 2.1 shard_map.149.gated_ref
  187.9 1.2 copy-done.4
  189.1 99.5 %shard_map.150 = bf16[16,64,1024]{2,1,0:T(8,128)(2,1)S(1)} custom-call(bf16[512,128]{1,0:T(8,128)(2,1)S(1)} %shard_map.149.gated_ref, bf16[4,512,256]{2,1,0:T(8,128)(2,1)S(1)} %copy-done.4, bf16[64,1024]{1,0:T(8,128)(2,1)S(1)} %bitcast.36, bf16[16,1024]{1,0:T(8,128)(2,1)S(1)} %pad_maximum_fusion.hot_ref, f32[8,1024]{1,0:T(8,128)S(1)} %broadcast_in_dim.29.gain_ref), custom_call_target="tpu_custom_call" | custom-call | flops 1100000000 | bytes 100000000 | tf_op jit(solution)/shard_map/pallas_call | solution.py:530
  288.6 3.5 %copy.28 = bf16[16,32,2,1024]{3,2,1,0:T(2,128)(2,1)} copy(bf16[16,32,2,1024]{3,1,2,0:T(8,128)(2,1)S(1)} %bitcast.32) | data formatting | bytes 4194304 | tf_op jit(solution)/shard_map/transpose | solution.py:639
  292.0 0.2 select_reduce_fusion
  292.2 0.4 convolution_convert_fusion.3
  292.6 0.8 copy.34
  293.4 2.7 fusion
  (43 shorter events, 0.3 us)
Async XLA Ops:
  0.6 184.4 %copy-start = (bf16[8,4,64]{2,1,0:T(4,128)(2,1)S(1)}, bf16[8,4,64]{2,1,0:T(4,128)(2,1)}, u32[]{:S(2)}) copy-start(bf16[8,4,64]{2,1,0:T(4,128)(2,1)} %param.19) | copy-start | bytes 12292
  0.6 19.2 %copy-start.5 = (bf16[256,8,128]{2,1,0:T(8,128)(2,1)S(1)}, bf16[256,8,128]{2,1,0:T(8,128)(2,1)}, u32[]{:S(2)}) copy-start(bf16[256,8,128]{2,1,0:T(8,128)(2,1)} %param.16) | copy-start | bytes 1572868
  4.6 44.3 %all-to-all-start.1 = ((bf16[16,64,256]{2,1,0:T(8,128)(2,1)}), bf16[16,64,256]{2,1,0:T(8,128)(2,1)S(1)}, u32[]{:S(2)}, u32[]{:S(2)}) async-start(bf16[16,64,256]{2,1,0:T(8,128)(2,1)} %copy.32), calls=%async_computation.1 | async-start | bytes 1048576 | tf_op jit(solution)/shard_map/all_to_all | solution.py:579
  20.4 34.9 %copy-start.11 = (s32[128]{0:T(128)S(1)}, s32[128]{0:T(128)}, u32[]{:S(2)}) copy-start(s32[128]{0:T(128)} %param.15) | copy-start | bytes 1540
  20.4 35.0 %copy-start.6 = (bf16[32,2,1024]{2,1,0:T(2,128)(2,1)S(1)}, bf16[32,2,1024]{2,1,0:T(2,128)(2,1)}, u32[]{:S(2)}) copy-start(bf16[32,2,1024]{2,1,0:T(2,128)(2,1)} %param.13) | copy-start | bytes 393220
  21.7 33.8 %copy-start.12 = (bf16[8]{0:T(256)(128)(2,1)S(1)}, bf16[8]{0:T(256)(128)(2,1)}, u32[]{:S(2)}) copy-start(bf16[8]{0:T(256)(128)(2,1)} %param.22) | copy-start | bytes 52
  21.7 35.1 %copy-start.7 = (bf16[256,8]{0,1:T(8,128)(2,1)S(1)}, bf16[256,8]{0,1:T(8,128)(2,1)}, u32[]{:S(2)}) copy-start(bf16[256,8]{0,1:T(8,128)(2,1)} %param.17) | copy-start | bytes 12292
  21.7 35.1 %copy-start.9 = (bf16[4,128]{1,0:T(4,128)(2,1)S(1)}, bf16[4,128]{1,0:T(4,128)(2,1)}, u32[]{:S(2)}) copy-start(bf16[4,128]{1,0:T(4,128)(2,1)} %param.20) | copy-start | bytes 3076
  21.7 35.1 %copy-start.1 = (bf16[8,64,256]{2,1,0:T(8,128)(2,1)S(1)}, bf16[8,64,256]{2,1,0:T(8,128)(2,1)}, u32[]{:S(2)}) copy-start(bf16[8,64,256]{2,1,0:T(8,128)(2,1)} %param.25) | copy-start | bytes 786436
  21.7 35.1 %copy-start.2 = (bf16[1024,128]{1,0:T(8,128)(2,1)S(1)}, bf16[1024,128]{1,0:T(8,128)(2,1)}, u32[]{:S(2)}) copy-start(bf16[1024,128]{1,0:T(8,128)(2,1)} %bc_ref.1) | copy-start | bytes 786436
  48.9 244.5 %all-to-all-start = ((bf16[16,256,128]{2,1,0:T(8,128)(2,1)}), bf16[16,256,128]{2,1,0:T(8,128)(2,1)}, u32[]{:S(2)}, u32[]{:S(2)}) async-start(bf16[16,256,128]{2,1,0:T(8,128)(2,1)} %copy.29), calls=%async_computation | async-start | bytes 2097152 | tf_op jit(solution)/shard_map/all_to_all | solution.py:579
  56.8 125.7 %copy-start.13 = (bf16[8]{0:T(256)(128)(2,1)S(1)}, bf16[8]{0:T(256)(128)(2,1)}, u32[]{:S(2)}) copy-start(bf16[8]{0:T(256)(128)(2,1)} %param.21) | copy-start | bytes 52
  56.8 127.0 %copy-start.14 = (bf16[8]{0:T(256)(128)(2,1)S(1)}, bf16[8]{0:T(256)(128)(2,1)}, u32[]{:S(2)}) copy-start(bf16[8]{0:T(256)(128)(2,1)} %param.23) | copy-start | bytes 52
  56.9 128.0 %copy-start.8 = (bf16[8,64]{1,0:T(8,128)(2,1)S(1)}, bf16[8,64]{1,0:T(8,128)(2,1)}, u32[]{:S(2)}) copy-start(bf16[8,64]{1,0:T(8,128)(2,1)} %param.24) | copy-start | bytes 3076
  181.4 1.0 copy-start.3
  187.8 1.2 copy-start.4
  288.5 3.5 %copy-start.10 = (s32[128]{0:T(128)S(1)}, s32[128]{0:T(128)}, u32[]{:S(2)}) copy-start(s32[128]{0:T(128)} %param.14) | copy-start | bytes 1540

commit v2 on v1

v2 whole, which is shorter than its diff:
```python
import jax
import jax.numpy as jnp
from jax import lax
from jax.experimental import pallas as pl
from jax.experimental.pallas import tpu as pltpu
from jax.sharding import PartitionSpec as P

STATE = 256
GROUP_HEADS = 32
KERNEL = 4
MESH = pl.DeviceIdType.MESH
NZ, NS, ND = 16, 8, 4
CHUNKS = 4
ROWS, WIDTH = 64 // CHUNKS, 1024 // CHUNKS
EARLY = (1, -1, 2, -2)
LATE = (3, -3, 4, -4, 5, -5, 6, -6, 7, -7, 8)
VMEM = pl.BlockSpec(memory_space=pltpu.VMEM)
SMEM = pl.BlockSpec(memory_space=pltpu.SMEM)
F32, BF16 = jnp.float32, jnp.bfloat16
ARRIVAL = (0, -1, 1, -2, 2, -3, 3, -4, 4, -5, 5, -6, 6, -7, 7, -8)


def place():
    return lax.axis_index("section"), lax.axis_index("tensor"), lax.axis_index("dp")


def turn(index, by, size):
    return lax.rem(index + (by % size), size)


def greet(peers):
    barrier = pltpu.get_barrier_semaphore()
    for peer in peers:
        pl.semaphore_signal(barrier, inc=1, device_id=peer, device_id_type=MESH)
    pl.semaphore_wait(barrier, len(peers))


def send(source, target, send_sem, recv_sem, peer):
    copy = pltpu.make_async_remote_copy(
        src_ref=source,
        dst_ref=target,
        send_sem=send_sem,
        recv_sem=recv_sem,
        device_id=peer,
        device_id_type=MESH,
    )
    copy.start()
    return copy


def dims(lhs, rhs):
    return (((lhs,), (rhs,)), ((), ()))


def layer_kernel(
    groups_ref, reads_ref, leaving_ref, origin_ref, scalars_ref,
    act_ref, xz_ref, dt_ref, bc_ref, out_ref, group_taps_ref, head_taps_ref, gain_ref,
    mixed_out, new_xz, new_rows,
    hot_ref, acts, weights, dts, rows_all, parts, parts_in, bc_parts, bc_in, step_parts, steps_in,
    bc_all, chosen, groups_in, xz_leaving, xz_coming, rows_leaving, rows_coming,
    own_gated, gathered, own_squares, squares_in, squares, z_squares, totals, product,
    right_out, right_in, left_out, left_in,
    w_send, w_recv, d_send, d_recv, o_send, o_recv, right_send, right_recv,
    left_send, left_recv, p_send, p_recv, b_send, b_recv, s_send, s_recv,
    z_send, z_recv, c_send, c_recv, e_send, e_recv, f_send, f_recv,
    g_send, g_recv, q_send, q_recv, u_send, u_recv, y_send, y_recv,
    sr_send, sr_recv, sl_send, sl_recv, gr_send, gr_recv, gl_send, gl_recv,
):
    s, t, d = place()
    right, left = (s, turn(t, 1, NZ), d), (s, turn(t, -1, NZ), d)
    sections = [turn(s, k, NS) for k in range(1, NS)]
    core = d + 1 - 2 * lax.rem(d, 2)
    across = turn(d, 2, ND)
    greet(
        [(s, turn(t, k, NZ), d) for k in range(1, NZ)]
        + [(p, t, d) for p in sections]
        + [(s, t, core), (s, t, across)]
    )
    sent = []

    def rows_at(index):
        return weights.at[pl.ds(pl.multiple_of(index * 256, 256), 256)]

    gathers = []

    def give(own, slot_of, ss, rs):
        near = send(own, slot_of(d), ss.at[0], rs.at[0], (s, t, core))
        far = send(own, slot_of(d), ss.at[1], rs.at[1], (s, t, across))
        sent.extend([near, far])
        gathers.append((slot_of, ss, rs, near, far))

    def start_ring(c):
        rows = pl.ds(ROWS * c, ROWS)
        return [
            send(act_ref.at[rows], acts.at[t, rows], right_send.at[0, c], right_recv.at[0, c], right),
            send(act_ref.at[rows], acts.at[t, rows], left_send.at[0, c], left_recv.at[0, c], left),
        ]

    rings = [start_ring(c) for c in range(CHUNKS)]
    for ring in rings:
        sent.extend(ring)
    own_rows = pl.ds(pl.multiple_of(d * 256, 256), 256)
    for h in range(NS):
        weights[own_rows, 128 * h : 128 * h + 128] = xz_ref[h]
    give(rows_at(d), rows_at, w_send, w_recv)
    give(dt_ref, lambda i: dts.at[i], d_send, d_recv)
    acts[t] = act_ref[...]
    dts[d] = dt_ref[...]
    rows_all[d] = out_ref[...].reshape(512, 256)
    lane = lax.broadcasted_iota(jnp.int32, (16, 128), 1)
    row = lax.rem(lax.broadcasted_iota(jnp.int32, (16, 128), 0), 8)
    halves = jnp.where(lane < 64, 0, 4)
    for h in range(NS):
        hot_ref[:, 128 * h : 128 * h + 128] = (row == halves + groups_ref[h]).astype(F32).astype(BF16)

    def pack(k):
        there = turn(t, k, NZ)
        if k == 0:
            xz_coming[t] = xz_ref[leaving_ref[there]]
            rows_coming[t] = out_ref[leaving_ref[there]]
        else:
            xz_leaving[k - 1] = xz_ref[leaving_ref[there]]
            rows_leaving[k - 1] = out_ref[leaving_ref[there]]

    for k in range(NZ):
        pack(k)
    moves = []

    def move(k):
        there = (s, turn(t, k, NZ), d)
        for source, target, ss, rs in (
            (xz_leaving, xz_coming, e_send, e_recv),
            (rows_leaving, rows_coming, f_send, f_recv),
        ):
            copy = send(source.at[k - 1], target.at[t], ss.at[k - 1], rs.at[k - 1], there)
            moves.append(copy)
            sent.append(copy)

    forwarded = []

    def forward_weights(which):
        slot_of, ss, rs, near, far = gathers[which]
        far.wait_recv()
        copy = send(slot_of(across), slot_of(across), ss.at[2], rs.at[2], (s, t, core))
        forwarded.append(copy)
        sent.append(copy)

    def have_weights(which):
        gathers[which][3].wait_recv()
        forwarded[which].wait_recv()

    def block_of(i):
        return turn(t, ARRIVAL[i], NZ)

    part_copies = []

    def project(group):
        rows = jnp.concatenate([acts[block_of(4 * group + i)] for i in range(4)], axis=0)
        for half in range(2):
            result = jnp.dot(
                rows, weights[:, 512 * half : 512 * half + 512], preferred_element_type=F32
            ).astype(BF16)
            for j in range(4):
                parts[4 * half + j, 4 * group : 4 * group + 4] = result[
                    :, 128 * j : 128 * j + 128
                ].reshape(4, 64, 128)
        for k in range(1, NS):
            span = pl.ds(4 * group, 4)
            copy = send(
                parts.at[sections[k - 1], span],
                parts_in.at[k - 1, span],
                p_send.at[k - 1, group],
                p_recv.at[k - 1, group],
                (sections[k - 1], t, d),
            )
            part_copies.append(copy)
            sent.append(copy)

    for step in range(1, 9):
        for c in range(CHUNKS):
            rows = pl.ds(ROWS * c, ROWS)
            rings[c][0].wait_recv()
            if step < 8:
                block = turn(t, -step, NZ)
                copy = send(
                    acts.at[block, rows], acts.at[block, rows],
                    right_send.at[step, c], right_recv.at[step, c], right,
                )
                rings[c][0] = copy
                sent.append(copy)
            if step < 8:
                rings[c][1].wait_recv()
            if step < 7:
                block = turn(t, step, NZ)
                copy = send(
                    acts.at[block, rows], acts.at[block, rows],
                    left_send.at[step, c], left_recv.at[step, c], left,
                )
                rings[c][1] = copy
                sent.append(copy)
        if step == 3:
            forward_weights(0)
            forward_weights(1)
        if step == 4:
            have_weights(0)
            have_weights(1)
            project(0)
        if step == 5:
            project(1)
        if step == 6:
            project(2)

    bc_parts[0] = jnp.zeros((64, 128), BF16)
    for i in range(4):
        result = jnp.dot(
            acts[4 * i : 4 * i + 4].reshape(256, 1024), bc_ref[...], preferred_element_type=F32
        )
        bc_parts[1 + 4 * i : 5 + 4 * i] = result.astype(BF16).reshape(4, 64, 128)
    bc_copies = []
    for k in range(1, NS):
        copy = send(
            bc_parts.at[pl.ds(2 * sections[k - 1], 3)],
            bc_in.at[k - 1],
            b_send.at[k - 1],
            b_recv.at[k - 1],
            (sections[k - 1], t, d),
        )
        bc_copies.append(copy)
        sent.append(copy)
    for k in EARLY:
        move(k % NZ)
    project(3)
    raw = jnp.zeros((16, 1024), F32)
    for i in range(ND):
        raw = raw + lax.dot_general(
            dts[i],
            acts[:, :, 256 * i : 256 * i + 256].reshape(1024, 256),
            dims(1, 1),
            preferred_element_type=F32,
        )
    for j in range(NS):
        for r in range(8):
            step_parts[j, r : r + 1, :] = raw[j : j + 1, 128 * r : 128 * r + 128]
    step_copies = []
    for k in range(1, NS):
        copy = send(
            step_parts.at[sections[k - 1]],
            steps_in.at[k - 1],
            s_send.at[k - 1],
            s_recv.at[k - 1],
            (sections[k - 1], t, d),
        )
        step_copies.append(copy)
        sent.append(copy)

    for copy in bc_copies:
        copy.wait_recv()
    total = bc_parts[pl.ds(2 * s, 3)].astype(F32)
    for k in range(NS - 1):
        total = total + bc_in[k].astype(F32)
    own_class, own_turn = 4 * lax.rem(t, 4), t // 4
    taps = group_taps_ref[...].astype(F32)
    for m in range(2):
        rows = total[:, 32 * m : 32 * m + 32, :].reshape(96, 128)
        u = jnp.zeros((64, 128), F32)
        for k in range(KERNEL):
            u = u + taps[k : k + 1, :] * rows[29 + k : 93 + k]
        u = (u / (1.0 + jnp.exp(-u))).astype(BF16)
        bc_all[own_class + own_turn, 32 * m : 32 * m + 32, :] = u[:32]
        bc_all[own_class + own_turn, 64 + 32 * m : 96 + 32 * m, :] = u[32:]

    def spread(copies, source, slot, by):
        copy = send(source, source, z_send.at[slot], z_recv.at[slot], (s, turn(t, by, NZ), d))
        copies.append(copy)
        sent.append(copy)

    copies = []
    for slot, by in enumerate((4, -4, 8)):
        spread(copies, bc_all.at[own_class + own_turn], slot, by)
    for copy in copies:
        copy.wait_recv()
    copies = []
    spread(copies, bc_all.at[pl.ds(own_class, 4)], 3, 1)
    spread(copies, bc_all.at[pl.ds(own_class, 4)], 4, -1)
    spread(copies, bc_all.at[own_class + own_turn], 5, 2)
    spread(copies, bc_all.at[own_class + turn(own_turn, 1, 4)], 6, 2)
    spread(copies, bc_all.at[own_class + turn(own_turn, 1, 4)], 7, -2)
    spread(copies, bc_all.at[own_class + turn(own_turn, 2, 4)], 8, -2)
    for copy in copies:
        copy.wait_recv()
    for k in LATE:
        move(k % NZ)

    def choose(section, j):
        return bc_all[reads_ref[4 * section + j]]

    choice_copies = []
    for k in range(1, NS):
        for j in range(4):
            chosen[k - 1, j] = choose(sections[k - 1], j)
        copy = send(
            chosen.at[k - 1], groups_in.at[s], c_send.at[k - 1], c_recv.at[k - 1],
            (sections[k - 1], t, d),
        )
        choice_copies.append(copy)
        sent.append(copy)
    for j in range(4):
        groups_in[s, j] = choose(s, j)
    give(rows_all.at[d], lambda i: rows_all.at[i], o_send, o_recv)

    for copy in part_copies + step_copies:
        copy.wait_recv()
    heads = [None] * NZ
    for i in range(NZ):
        value = parts[s, i].astype(F32)
        for k in range(NS - 1):
            value = value + parts_in[k, i].astype(F32)
        product[block_of(i), :, 0:128] = value
    raw = step_parts[s]
    for k in range(NS - 1):
        raw = raw + steps_in[k]

    raw = jnp.concatenate(
        [
            jnp.concatenate(
                [raw[2 * c + i // 2 : 2 * c + i // 2 + 1, 64 * (i % 2) + 32 * m : 64 * (i % 2) + 32 * m + 32]
                 for i in range(4)],
                axis=1,
            )
            for m in range(2)
            for c in range(4)
        ],
        axis=0,
    )
    raw = raw + scalars_ref[8 + s]
    step = jnp.maximum(raw, 0.0) + jnp.log1p(jnp.exp(-jnp.abs(raw)))
    log_decay = -step * jnp.exp(jnp.full((8, 128), scalars_ref[s], F32))
    skip = scalars_ref[16 + s]
    taps = head_taps_ref[s].astype(F32)
    taps = jnp.concatenate([taps, taps], axis=1)
    lane = lax.broadcasted_iota(jnp.int32, (128, 128), 1)
    row = lax.broadcasted_iota(jnp.int32, (128, 128), 0)
    causal = row >= lane
    upto = (row <= lane).astype(F32)
    same = (row == lane).astype(F32)
    exact = lax.Precision.HIGHEST
    cum = jnp.dot(log_decay, upto, precision=exact, preferred_element_type=F32)
    both = jnp.concatenate([cum, step], axis=0)
    columns = lax.dot_general(same, both, dims(1, 1), precision=exact, preferred_element_type=F32)
    tall = lax.broadcasted_iota(jnp.int32, (512, 128), 0)
    for copy in choice_copies:
        copy.wait_recv()
    gated = []
    for m in range(2):
        v = product[:, 32 * m : 32 * m + 32, 0:128].reshape(512, 128)
        u = taps[3:4, :] * v
        for back in range(1, KERNEL):
            moved = jnp.where(tall >= back, pltpu.roll(v, back, 0), 0.0)
            u = u + taps[3 - back : 4 - back, :] * moved
        x = (u / (1.0 + jnp.exp(-u))).astype(BF16)
        state = jnp.zeros((STATE, 128), F32)
        outs = []
        for c in range(4):
            at = 4 * m + c

            def pick(j):
                part = groups_in[2 * c : 2 * c + 2, j].reshape(2, 2, 2, 32, 128)
                return part[:, :, m].reshape(128, 128)

            b = jnp.concatenate([pick(0), pick(1)], axis=1)
            cc = jnp.concatenate([pick(2), pick(3)], axis=1)
            xc = x[128 * c : 128 * c + 128]
            xf = xc.astype(F32)
            cum_c, step_c = columns[:, at : at + 1], columns[:, 8 + at : 9 + at]
            cum_r, step_r = cum[at : at + 1, :], step[at : at + 1, :]
            scores = lax.dot_general(cc, b, dims(1, 1), preferred_element_type=F32)
            mixing = jnp.exp(jnp.where(causal, cum_c - cum_r, -1e30)) * step_r
            y = jnp.dot((scores * mixing).astype(BF16), xc, preferred_element_type=F32)
            y = y + jnp.exp(cum_c) * jnp.dot(cc, state.astype(BF16), preferred_element_type=F32)
            y = y + skip * xf
            outs.append(y)
            if c < 3:
                end = cum[at : at + 1, 127:128]
                tail = (jnp.exp(end - cum_c) * step_c * xf).astype(BF16)
                state = jnp.exp(end) * state + lax.dot_general(
                    b, tail, dims(0, 0), preferred_element_type=F32
                )
        z = pltpu.roll(v, 64, 1)
        gated.append(jnp.concatenate(outs, axis=0) * (z / (1.0 + jnp.exp(-z))))
    wide = lax.broadcasted_iota(jnp.int32, (512, 128), 1)
    packed = jnp.where(wide < 64, gated[0], pltpu.roll(gated[1], 64, 1))
    own_gated[...] = packed.astype(BF16)

    y = lax.rem(s, 4)
    own_hot = hot_ref[:, pl.ds(pl.multiple_of(128 * s, 128), 128)]
    for j in range(4):
        part = packed[128 * j : 128 * j + 128]
        own_squares[j] = lax.dot_general(
            own_hot, (part * part).astype(BF16), dims(1, 1), preferred_element_type=F32
        )[:8]
    square_copies = []
    for k in range(1, NS):
        copy = send(
            own_squares.at[lax.rem(sections[k - 1], 4)], squares_in.at[k - 1],
            u_send.at[k - 1], u_recv.at[k - 1], (sections[k - 1], t, d),
        )
        square_copies.append(copy)
        sent.append(copy)
    gather_copies = []
    for k in range(1, NS):
        copy = send(
            own_gated, gathered.at[s], g_send.at[k - 1], g_recv.at[k - 1], (sections[k - 1], t, d)
        )
        gather_copies.append(copy)
        sent.append(copy)
    gathered[s] = own_gated[...]
    for copy in square_copies:
        copy.wait_recv()
    value = own_squares[y]
    for k in range(NS - 1):
        value = value + squares_in[k]
    squares[...] = value
    copies = []
    for k in range(1, NZ):
        copy = send(
            squares, z_squares.at[k - 1], q_send.at[k - 1], q_recv.at[k - 1],
            (s, turn(t, k, NZ), d),
        )
        copies.append(copy)
        sent.append(copy)
    for copy in copies:
        copy.wait_recv()
    for k in range(NZ - 1):
        value = value + z_squares[k]
    totals[y] = value
    copies = []
    for k in range(1, 4):
        copy = send(
            totals.at[y], totals.at[y], y_send.at[k - 1], y_recv.at[k - 1],
            (s - y + turn(y, k, 4), t, d),
        )
        copies.append(copy)
        sent.append(copy)
    forward_weights(2)
    for copy in copies + gather_copies:
        copy.wait_recv()
    have_weights(2)

    wide = lax.broadcasted_iota(jnp.int32, (128, 128), 1)
    gain = gain_ref[...].astype(F32)
    gain = jnp.concatenate([gain, gain], axis=1)
    for j in range(4):
        inverse = lax.rsqrt(totals[j] / (GROUP_HEADS * 64) + 1e-05)
        high = inverse.astype(BF16)
        low = (inverse - high.astype(F32)).astype(BF16)
        scale = lax.dot_general(
            jnp.concatenate([high, low], axis=0), hot_ref[...], dims(0, 0),
            preferred_element_type=F32,
        )
        first, second = [], []
        for i in range(0, NS, 2):
            pair = []
            for h in (i, i + 1):
                span = slice(128 * h, 128 * h + 128)
                value = gathered[h, 128 * j : 128 * j + 128, :].astype(F32)
                pair.append(value * scale[:, span] * gain[h : h + 1, :])
            even, odd = pair
            first.append(jnp.where(wide < 64, even, pltpu.roll(odd, 64, 1)).astype(BF16))
            second.append(jnp.where(wide < 64, pltpu.roll(even, 64, 1), odd).astype(BF16))
        lhs = jnp.concatenate(
            [jnp.concatenate(first, axis=1), jnp.concatenate(second, axis=1)], axis=0
        )
        for i in range(ND):
            result = jnp.dot(lhs, rows_all[i], preferred_element_type=F32)
            for m in range(2):
                product[
                    4 * j : 4 * j + 4, 32 * m : 32 * m + 32, 256 * i : 256 * i + 256
                ] = result[128 * m : 128 * m + 128].reshape(4, 32, 256)

    from_left, from_right = [None] * CHUNKS, [None] * CHUNKS
    for step in range(8):
        for h in range(CHUNKS):
            span = slice(WIDTH * h, WIDTH * h + WIDTH)
            value = product[turn(t, 8 - step, NZ), :, span]
            if step > 0:
                from_left[h].wait_recv()
                value = value + right_in[step - 1, h].astype(F32)
            right_out[step, h] = value.astype(BF16)
            from_left[h] = send(
                right_out.at[step, h], right_in.at[step, h],
                sr_send.at[step, h], sr_recv.at[step, h], right,
            )
            sent.append(from_left[h])
            if step < 7:
                value = product[turn(t, step - 7, NZ), :, span]
                if step > 0:
                    from_right[h].wait_recv()
                    value = value + left_in[step - 1, h].astype(F32)
                left_out[step, h] = value.astype(BF16)
                from_right[h] = send(
                    left_out.at[step, h], left_in.at[step, h],
                    sl_send.at[step, h], sl_recv.at[step, h], left,
                )
                sent.append(from_right[h])
    for h in range(CHUNKS):
        span = slice(WIDTH * h, WIDTH * h + WIDTH)
        from_left[h].wait_recv()
        from_right[h].wait_recv()
        value = product[t, :, span] + act_ref[:, span].astype(F32)
        value = value + right_in[7, h].astype(F32) + left_in[6, h].astype(F32)
        mixed_out[t, :, span] = value.astype(BF16)

    rings = [[None, None] for _ in range(CHUNKS)]
    for step in range(9):
        for c in range(CHUNKS):
            rows = pl.ds(ROWS * c, ROWS)
            if step > 0:
                rings[c][0].wait_recv()
            if step < 8:
                block = turn(t, -step, NZ)
                rings[c][0] = send(
                    mixed_out.at[block, rows], mixed_out.at[block, rows],
                    gr_send.at[step, c], gr_recv.at[step, c], right,
                )
                sent.append(rings[c][0])
            if 0 < step < 8:
                rings[c][1].wait_recv()
            if step < 7:
                block = turn(t, step, NZ)
                rings[c][1] = send(
                    mixed_out.at[block, rows], mixed_out.at[block, rows],
                    gl_send.at[step, c], gl_recv.at[step, c], left,
                )
                sent.append(rings[c][1])
        if step == 0:
            for copy in moves:
                copy.wait_recv()
            for k in range(NS):
                new_xz[:, 128 * k : 128 * k + 128] = xz_coming[origin_ref[k]]
                new_rows[64 * k : 64 * k + 64, :] = rows_coming[origin_ref[k]]
    for copy in sent:
        copy.wait_send()


def layer_call(*operands):
    def dma(*shape):
        return [pltpu.SemaphoreType.DMA(shape)] * 2

    return pl.pallas_call(
        layer_kernel,
        out_shape=(
            jax.ShapeDtypeStruct((NZ, 64, 1024), BF16),
            jax.ShapeDtypeStruct((256, 1024), BF16),
            jax.ShapeDtypeStruct((512, 256), BF16),
        ),
        in_specs=[SMEM] * 5 + [VMEM] * 8,
        out_specs=(VMEM,) * 3,
        scratch_shapes=[
            pltpu.VMEM((16, 1024), BF16),
            pltpu.VMEM((NZ, 64, 1024), BF16),
            pltpu.VMEM((1024, 1024), BF16),
            pltpu.VMEM((ND, 16, 256), BF16),
            pltpu.VMEM((ND, 512, 256), BF16),
            pltpu.VMEM((NS, NZ, 64, 128), BF16),
            pltpu.VMEM((NS - 1, NZ, 64, 128), BF16),
            pltpu.VMEM((NZ + 1, 64, 128), BF16),
            pltpu.VMEM((NS - 1, 3, 64, 128), BF16),
            pltpu.VMEM((NS, 8, 128), F32),
            pltpu.VMEM((NS - 1, 8, 128), F32),
            pltpu.VMEM((NZ, 128, 128), BF16),
            pltpu.VMEM((NS - 1, 4, 128, 128), BF16),
            pltpu.VMEM((NS, 4, 128, 128), BF16),
            pltpu.VMEM((NZ - 1, 256, 128), BF16),
            pltpu.VMEM((NZ, 256, 128), BF16),
            pltpu.VMEM((NZ - 1, 64, 256), BF16),
            pltpu.VMEM((NZ, 64, 256), BF16),
            pltpu.VMEM((512, 128), BF16),
            pltpu.VMEM((NS, 512, 128), BF16),
            pltpu.VMEM((4, 8, 128), F32),
            pltpu.VMEM((NS - 1, 8, 128), F32),
            pltpu.VMEM((8, 128), F32),
            pltpu.VMEM((NZ - 1, 8, 128), F32),
            pltpu.VMEM((4, 8, 128), F32),
            pltpu.VMEM((NZ, 64, 1024), F32),
            pltpu.VMEM((8, CHUNKS, 64, WIDTH), BF16),
            pltpu.VMEM((8, CHUNKS, 64, WIDTH), BF16),
            pltpu.VMEM((7, CHUNKS, 64, WIDTH), BF16),
            pltpu.VMEM((7, CHUNKS, 64, WIDTH), BF16),
            *dma(3), *dma(3), *dma(3),
            *dma(8, CHUNKS), *dma(7, CHUNKS),
            *dma(NS - 1, 4), *dma(NS - 1), *dma(NS - 1),
            *dma(9), *dma(NS - 1), *dma(NZ - 1), *dma(NZ - 1),
            *dma(NS - 1), *dma(NZ - 1), *dma(NS - 1), *dma(3),
            *dma(8, CHUNKS), *dma(7, CHUNKS), *dma(8, CHUNKS), *dma(7, CHUNKS),
        ],
        compiler_params=pltpu.CompilerParams(
            collective_id=0, has_side_effects=True, vmem_limit_bytes=36 << 20
        ),
        cost_estimate=pl.CostEstimate(
            flops=4_000_000_000, bytes_accessed=100_000_000, transcendentals=0
        ),
    )(*operands)


def head_maps(old_heads, new_heads, member):
    both = jnp.stack([old_heads, new_heads]).reshape(2, NZ, NS)
    mine = lax.dynamic_index_in_dim(both, member, 1, keepdims=False)
    groups = mine[0] // GROUP_HEADS
    j = jnp.arange(4, dtype=jnp.int32)
    block = 8 * (j // 2) + 2 * groups[:, None] + j % 2
    reads = (4 * (block % 4) + block // 4).reshape(4 * NS)
    slots = jnp.arange(NS, dtype=jnp.int32)
    devices = jnp.arange(NZ, dtype=jnp.int32)
    leaving = jnp.sum(
        jnp.where(both[1][:, :, None] == mine[0], slots, 0), axis=(1, 2), dtype=jnp.int32
    )
    origin = jnp.sum(
        jnp.where(both[0][:, :, None] == mine[1], devices[:, None, None], 0),
        axis=(0, 1),
        dtype=jnp.int32,
    )
    return groups, reads, leaving, origin


def per_device(
    activations,
    old_heads,
    new_heads,
    xz_weight,
    dt_weight,
    bc_weight,
    conv_heads,
    conv_groups,
    decay_log,
    dt_bias,
    skip_gain,
    norm_gain,
    out_weight,
):
    _, t, _ = place()
    groups, reads, leaving, origin = head_maps(old_heads, new_heads, t)
    mixed, new_xz, new_out = layer_call(
        groups,
        reads,
        leaving,
        origin,
        jnp.concatenate([decay_log, dt_bias, skip_gain]).astype(F32),
        jnp.transpose(activations, (1, 0, 2)).reshape(64, 1024),
        jnp.transpose(xz_weight, (1, 0, 2)),
        jnp.pad(jnp.transpose(dt_weight), ((0, 8), (0, 0))),
        bc_weight,
        out_weight,
        conv_groups,
        conv_heads,
        norm_gain,
    )
    mixed = jnp.transpose(mixed.reshape(16, 2, 32, 1024), (0, 2, 1, 3)).reshape(512, 2, 1024)
    return mixed, new_xz.reshape(256, 8, 128), new_out.reshape(8, 64, 256)


def solution(mesh):
    in_specs = (
        P("tensor", "dp", "section"),
        P(),
        P(),
        P(("section", "dp"), "tensor", None),
        P(("section", "dp"), "tensor"),
        P("section", "tensor"),
        P("tensor", None, None),
        P(None, "tensor"),
        P("tensor"),
        P("tensor"),
        P("tensor"),
        P("tensor", None),
        P("tensor", None, ("section", "dp")),
    )
    out_specs = (
        P(None, "dp", "section"),
        P(("section", "dp"), "tensor", None),
        P("tensor", None, ("section", "dp")),
    )
    return jax.shard_map(
        per_device, mesh=mesh, in_specs=in_specs, out_specs=out_specs, check_vma=False
    )
```

time: 302 us -> 227 us (0.75); the launches traced: 296 us -> 225 us
  waiting for transfers between devices: 27.2 us -> 0 us
  starting transfers between devices: 21.5 us -> 0 us
  Pallas kernels: 226 us -> 208 us
  matrix products: 5.01 us -> 0 us
  local copies, waits for them, and re-layouts: 11.2 us -> 15 us
    all_to_all x2 -> x0, waiting for transfers between devices: 27.2 us -> none  [exchange(): lax.all_to_all(array, 'tensor', split_axis=0, concat_axis=0, tiled=True)]
    all_to_all x2 -> x0, starting transfers between devices: 21.5 us -> none  [exchange(): lax.all_to_all(array, 'tensor', split_axis=0, concat_axis=0, tiled=True)]
    pallas_call x3 -> x1, Pallas kernels: 226 us -> 208 us  [layer_call(): pl.pallas_call(layer_kernel, out_shape=(jax.ShapeDtypeStruct((NZ, 64, 102...]
    dot_general x4 -> x0, matrix products: 5.01 us -> none  [select(): jnp.einsum(form, mask, array, preferred_element_type=F32).astype(BF16)]
    unnamed x32 -> x13, local copies, waits for them, and re-layouts: 3.12 us -> 6.66 us
  transfers between devices with their start and end apart: 2 -> 0, of which waited for: 1 -> 0; matrix products, arithmetic and copies ran while one was open for 3% -> 0% of each run, Pallas kernels for 76% -> 0%
where the time goes in v2:
time: 227 us; the launch traced here: 225 us
  Pallas kernels  208 us (92%)
  local copies, waits for them, and re-layouts  15 us (7%)
    pallas_call x1, Pallas kernels, layer_call(): pl.pallas_call(layer_kernel, out_shape=(jax.ShapeDtypeStruct((NZ, 64, 102...  208 us
    unnamed x13, local copies, waits for them, and re-layouts  6.66 us

profile of v2, /device:TPU:6, one launch (start us, length us, event | category | flops | bytes accessed | tf_op | source)
XLA Modules:
  0.0 225.2 jit_solution(7312233812611141775)
XLA Ops:
  0.6 0.8 maximum_convert_fusion.scalars_ref
  1.4 0.7 pad.4.dt_ref
  2.1 0.7 eq.40
  2.8 0.1 copy.23
  2.9 0.7 stack.9
  3.6 0.7 eq.36
  4.4 0.1 copy.22
  4.5 0.7 stack.10
  5.3 0.2 select_reduce_fusion
  5.4 0.1 add_add_fusion
  5.5 0.1 add.73
  5.6 0.9 copy.24
  6.6 1.1 copy.29
  7.7 0.0 copy-start
  7.7 0.9 copy-done
  8.6 0.0 copy-start.1
  8.6 0.9 copy-done.1
  9.6 0.0 copy-start.2
  9.6 0.7 copy-done.2
  10.3 0.0 copy-start.3
  10.3 0.7 copy-done.3
  11.0 0.0 copy-start.4
  11.0 0.7 copy-done.4
  11.6 208.5 %shard_map.148 = (bf16[16,64,1024]{2,1,0:T(8,128)(2,1)S(1)}, bf16[256,1024]{1,0:T(8,128)(2,1)S(1)}, bf16[512,256]{1,0:T(8,128)(2,1)S(1)}) custom-call(s32[8]{0:T(128)S(1)} %get-tuple-element.10.groups_ref, s32[32]{0:T(128)S(1)} %fusion.3.reads_ref, s32[16]{0:T(128)S(1)} %get-tuple-element.16.leaving_ref, s32[8]{0:T(128)S(1)} %get-tuple-element.15.origin_ref, ...), custom_call_target="tpu_custom_call" | custom-call | flops 4000000000 | bytes 100000000 | tf_op jit(solution)/shard_map/pallas_call | solution.py:549
  220.1 3.5 %copy.26 = bf16[16,32,2,1024]{3,2,1,0:T(2,128)(2,1)} copy(bf16[16,32,2,1024]{3,1,2,0:T(8,128)(2,1)S(1)} %bitcast.20) | data formatting | bytes 4194304 | tf_op jit(solution)/shard_map/transpose | solution.py:657
  223.6 0.9 copy.27
  224.5 0.7 copy.31
  (5 shorter events, 0.0 us)
Async XLA Ops:
  7.7 1.0 copy-start
  8.6 0.9 copy-start.1
  9.6 0.7 copy-start.2
  10.3 0.7 copy-start.3
  11.0 0.7 copy-start.4

commit v3 on v2

--- a/solution.py
+++ b/solution.py
@@ -11,11 +11,12 @@
 MESH = pl.DeviceIdType.MESH
 NZ, NS, ND = 16, 8, 4
 CHUNKS = 4
-ROWS, WIDTH = 64 // CHUNKS, 1024 // CHUNKS
-EARLY = (1, -1, 2, -2)
-LATE = (3, -3, 4, -4, 5, -5, 6, -6, 7, -7, 8)
+WIDTH = 1024 // CHUNKS
+WHOLE = ((8,), (1, -1, 2, -2, 3, -3), (7, -7, 6, -6, 5, -5))
+PIECES = ((), (4, -4), ())
 VMEM = pl.BlockSpec(memory_space=pltpu.VMEM)
 SMEM = pl.BlockSpec(memory_space=pltpu.SMEM)
+HBM = pl.BlockSpec(memory_space=pltpu.HBM)
 F32, BF16 = jnp.float32, jnp.bfloat16
 ARRIVAL = (0, -1, 1, -2, 2, -3, 3, -4, 4, -5, 5, -6, 6, -7, 7, -8)
 
@@ -54,8 +55,9 @@
 
 def layer_kernel(
     groups_ref, reads_ref, leaving_ref, origin_ref, scalars_ref,
-    act_ref, xz_ref, dt_ref, bc_ref, out_ref, group_taps_ref, head_taps_ref, gain_ref,
+    act_ref, xz_ref, dt_ref, bc_hbm, out_hbm, group_taps_hbm, head_taps_hbm, gain_hbm,
     mixed_out, new_xz, new_rows,
+    bc_ref, out_ref, group_taps_ref, head_taps_ref, gain_ref, load_sem,
     hot_ref, acts, weights, dts, rows_all, parts, parts_in, bc_parts, bc_in, step_parts, steps_in,
     bc_all, chosen, groups_in, xz_leaving, xz_coming, rows_leaving, rows_coming,
     own_gated, gathered, own_squares, squares_in, squares, z_squares, totals, product,
@@ -71,6 +73,20 @@
     sections = [turn(s, k, NS) for k in range(1, NS)]
     core = d + 1 - 2 * lax.rem(d, 2)
     across = turn(d, 2, ND)
+    loads = [
+        pltpu.make_async_copy(source, target, load_sem.at[i])
+        for i, (source, target) in enumerate(
+            (
+                (out_hbm, out_ref),
+                (bc_hbm, bc_ref),
+                (group_taps_hbm, group_taps_ref),
+                (head_taps_hbm, head_taps_ref),
+                (gain_hbm, gain_ref),
+            )
+        )
+    ]
+    for load in loads:
+        load.start()
     greet(
         [(s, turn(t, k, NZ), d) for k in range(1, NZ)]
         + [(p, t, d) for p in sections]
@@ -90,10 +106,10 @@
         gathers.append((slot_of, ss, rs, near, far))
 
     def start_ring(c):
-        rows = pl.ds(ROWS * c, ROWS)
+        span = pl.ds(WIDTH * c, WIDTH)
         return [
-            send(act_ref.at[rows], acts.at[t, rows], right_send.at[0, c], right_recv.at[0, c], right),
-            send(act_ref.at[rows], acts.at[t, rows], left_send.at[0, c], left_recv.at[0, c], left),
+            send(act_ref.at[:, span], acts.at[t, :, span], right_send.at[0, c], right_recv.at[0, c], right),
+            send(act_ref.at[:, span], acts.at[t, :, span], left_send.at[0, c], left_recv.at[0, c], left),
         ]
 
     rings = [start_ring(c) for c in range(CHUNKS)]
@@ -106,6 +122,8 @@
     give(dt_ref, lambda i: dts.at[i], d_send, d_recv)
     acts[t] = act_ref[...]
     dts[d] = dt_ref[...]
+    for load in loads:
+        load.wait()
     rows_all[d] = out_ref[...].reshape(512, 256)
     lane = lax.broadcasted_iota(jnp.int32, (16, 128), 1)
     row = lax.rem(lax.broadcasted_iota(jnp.int32, (16, 128), 0), 8)
@@ -126,16 +144,38 @@
         pack(k)
     moves = []
 
-    def move(k):
+    def move(k, piece=None):
         there = (s, turn(t, k, NZ), d)
-        for source, target, ss, rs in (
-            (xz_leaving, xz_coming, e_send, e_recv),
-            (rows_leaving, rows_coming, f_send, f_recv),
-        ):
-            copy = send(source.at[k - 1], target.at[t], ss.at[k - 1], rs.at[k - 1], there)
+        parts_of = []
+        if piece is None:
+            parts_of.append((xz_leaving.at[k - 1], xz_coming.at[t], e_send.at[k - 1, 0], e_recv.at[k - 1, 0]))
+            parts_of.append((rows_leaving.at[k - 1], rows_coming.at[t], f_send.at[k - 1, 0], f_recv.at[k - 1, 0]))
+        elif piece < 4:
+            rows = pl.ds(64 * piece, 64)
+            parts_of.append(
+                (xz_leaving.at[k - 1, rows], xz_coming.at[t, rows], e_send.at[k - 1, piece], e_recv.at[k - 1, piece])
+            )
+        else:
+            half = piece - 4
+            rows = pl.ds(32 * half, 32)
+            parts_of.append(
+                (rows_leaving.at[k - 1, rows], rows_coming.at[t, rows], f_send.at[k - 1, half], f_recv.at[k - 1, half])
+            )
+        for source, target, ss, rs in parts_of:
+            copy = send(source, target, ss, rs, there)
             moves.append(copy)
             sent.append(copy)
 
+    def move_whole(point):
+        for k in WHOLE[point]:
+            move(k % NZ)
+
+    def move_pieces(ring, step):
+        for k in PIECES[ring]:
+            if step < 6:
+                move(k % NZ, step)
+
+    move_whole(0)
     forwarded = []
 
     def forward_weights(which):
@@ -178,12 +218,12 @@
 
     for step in range(1, 9):
         for c in range(CHUNKS):
-            rows = pl.ds(ROWS * c, ROWS)
+            span = pl.ds(WIDTH * c, WIDTH)
             rings[c][0].wait_recv()
             if step < 8:
                 block = turn(t, -step, NZ)
                 copy = send(
-                    acts.at[block, rows], acts.at[block, rows],
+                    acts.at[block, :, span], acts.at[block, :, span],
                     right_send.at[step, c], right_recv.at[step, c], right,
                 )
                 rings[c][0] = copy
@@ -193,11 +233,12 @@
             if step < 7:
                 block = turn(t, step, NZ)
                 copy = send(
-                    acts.at[block, rows], acts.at[block, rows],
+                    acts.at[block, :, span], acts.at[block, :, span],
                     left_send.at[step, c], left_recv.at[step, c], left,
                 )
                 rings[c][1] = copy
                 sent.append(copy)
+        move_pieces(0, step - 1)
         if step == 3:
             forward_weights(0)
             forward_weights(1)
@@ -207,8 +248,6 @@
             project(0)
         if step == 5:
             project(1)
-        if step == 6:
-            project(2)
 
     bc_parts[0] = jnp.zeros((64, 128), BF16)
     for i in range(4):
@@ -227,8 +266,8 @@
         )
         bc_copies.append(copy)
         sent.append(copy)
-    for k in EARLY:
-        move(k % NZ)
+    move_whole(1)
+    project(2)
     project(3)
     raw = jnp.zeros((16, 1024), F32)
     for i in range(ND):
@@ -274,9 +313,19 @@
         copies.append(copy)
         sent.append(copy)
 
+    def gather_parts(start, stop):
+        for i in range(start, stop):
+            value = parts[s, i].astype(F32)
+            for k in range(NS - 1):
+                value = value + parts_in[k, i].astype(F32)
+            product[block_of(i), :, 0:128] = value
+
     copies = []
     for slot, by in enumerate((4, -4, 8)):
         spread(copies, bc_all.at[own_class + own_turn], slot, by)
+    for copy in part_copies[: 2 * NS - 2]:
+        copy.wait_recv()
+    gather_parts(0, 8)
     for copy in copies:
         copy.wait_recv()
     copies = []
@@ -288,8 +337,7 @@
     spread(copies, bc_all.at[own_class + turn(own_turn, 2, 4)], 8, -2)
     for copy in copies:
         copy.wait_recv()
-    for k in LATE:
-        move(k % NZ)
+    move_whole(2)
 
     def choose(section, j):
         return bc_all[reads_ref[4 * section + j]]
@@ -308,14 +356,9 @@
         groups_in[s, j] = choose(s, j)
     give(rows_all.at[d], lambda i: rows_all.at[i], o_send, o_recv)
 
-    for copy in part_copies + step_copies:
-        copy.wait_recv()
-    heads = [None] * NZ
-    for i in range(NZ):
-        value = parts[s, i].astype(F32)
-        for k in range(NS - 1):
-            value = value + parts_in[k, i].astype(F32)
-        product[block_of(i), :, 0:128] = value
+    for copy in part_copies[2 * NS - 2 :] + step_copies:
+        copy.wait_recv()
+    gather_parts(8, NZ)
     raw = step_parts[s]
     for k in range(NS - 1):
         raw = raw + steps_in[k]
@@ -449,8 +492,9 @@
     wide = lax.broadcasted_iota(jnp.int32, (128, 128), 1)
     gain = gain_ref[...].astype(F32)
     gain = jnp.concatenate([gain, gain], axis=1)
-    for j in range(4):
-        inverse = lax.rsqrt(totals[j] / (GROUP_HEADS * 64) + 1e-05)
+
+    def multiply(tile):
+        inverse = lax.rsqrt(totals[tile] / (GROUP_HEADS * 64) + 1e-05)
         high = inverse.astype(BF16)
         low = (inverse - high.astype(F32)).astype(BF16)
         scale = lax.dot_general(
@@ -462,7 +506,7 @@
             pair = []
             for h in (i, i + 1):
                 span = slice(128 * h, 128 * h + 128)
-                value = gathered[h, 128 * j : 128 * j + 128, :].astype(F32)
+                value = gathered[h, pl.ds(pl.multiple_of(128 * tile, 128), 128), :].astype(F32)
                 pair.append(value * scale[:, span] * gain[h : h + 1, :])
             even, odd = pair
             first.append(jnp.where(wide < 64, even, pltpu.roll(odd, 64, 1)).astype(BF16))
@@ -474,11 +518,18 @@
             result = jnp.dot(lhs, rows_all[i], preferred_element_type=F32)
             for m in range(2):
                 product[
-                    4 * j : 4 * j + 4, 32 * m : 32 * m + 32, 256 * i : 256 * i + 256
+                    pl.ds(4 * tile, 4), 32 * m : 32 * m + 32, 256 * i : 256 * i + 256
                 ] = result[128 * m : 128 * m + 128].reshape(4, 32, 256)
+
+    first_tile = turn(t, 8, NZ) // 4
+    for i in range(2):
+        multiply(turn(first_tile, i, 4))
 
     from_left, from_right = [None] * CHUNKS, [None] * CHUNKS
     for step in range(8):
+        if step == 1:
+            for i in range(2, 4):
+                multiply(turn(first_tile, i, 4))
         for h in range(CHUNKS):
             span = slice(WIDTH * h, WIDTH * h + WIDTH)
             value = product[turn(t, 8 - step, NZ), :, span]
@@ -502,6 +553,8 @@
                     sl_send.at[step, h], sl_recv.at[step, h], left,
                 )
                 sent.append(from_right[h])
+        move_pieces(1, step)
+    rings = []
     for h in range(CHUNKS):
         span = slice(WIDTH * h, WIDTH * h + WIDTH)
         from_left[h].wait_recv()
@@ -509,30 +562,38 @@
         value = product[t, :, span] + act_ref[:, span].astype(F32)
         value = value + right_in[7, h].astype(F32) + left_in[6, h].astype(F32)
         mixed_out[t, :, span] = value.astype(BF16)
-
-    rings = [[None, None] for _ in range(CHUNKS)]
-    for step in range(9):
+        span = pl.ds(WIDTH * h, WIDTH)
+        ring = []
+        for ss, rs, peer in ((gr_send, gr_recv, right), (gl_send, gl_recv, left)):
+            ring.append(
+                send(mixed_out.at[t, :, span], mixed_out.at[t, :, span], ss.at[0, h], rs.at[0, h], peer)
+            )
+        sent.extend(ring)
+        rings.append(ring)
+
+    move_pieces(2, 0)
+    for step in range(1, 9):
         for c in range(CHUNKS):
-            rows = pl.ds(ROWS * c, ROWS)
-            if step > 0:
-                rings[c][0].wait_recv()
+            span = pl.ds(WIDTH * c, WIDTH)
+            rings[c][0].wait_recv()
             if step < 8:
                 block = turn(t, -step, NZ)
                 rings[c][0] = send(
-                    mixed_out.at[block, rows], mixed_out.at[block, rows],
+                    mixed_out.at[block, :, span], mixed_out.at[block, :, span],
                     gr_send.at[step, c], gr_recv.at[step, c], right,
                 )
                 sent.append(rings[c][0])
-            if 0 < step < 8:
+            if step < 8:
                 rings[c][1].wait_recv()
             if step < 7:
                 block = turn(t, step, NZ)
                 rings[c][1] = send(
-                    mixed_out.at[block, rows], mixed_out.at[block, rows],
+                    mixed_out.at[block, :, span], mixed_out.at[block, :, span],
                     gl_send.at[step, c], gl_recv.at[step, c], left,
                 )
                 sent.append(rings[c][1])
-        if step == 0:
+        move_pieces(2, step)
+        if step == 7:
             for copy in moves:
                 copy.wait_recv()
             for k in range(NS):
@@ -553,9 +614,15 @@
             jax.ShapeDtypeStruct((256, 1024), BF16),
             jax.ShapeDtypeStruct((512, 256), BF16),
         ),
-        in_specs=[SMEM] * 5 + [VMEM] * 8,
+        in_specs=[SMEM] * 5 + [VMEM] * 3 + [HBM] * 5,
         out_specs=(VMEM,) * 3,
         scratch_shapes=[
+            pltpu.VMEM((1024, 128), BF16),
+            pltpu.VMEM((NS, 64, 256), BF16),
+            pltpu.VMEM((KERNEL, 128), BF16),
+            pltpu.VMEM((NS, KERNEL, 64), BF16),
+            pltpu.VMEM((NS, 64), BF16),
+            pltpu.SemaphoreType.DMA((5,)),
             pltpu.VMEM((16, 1024), BF16),
             pltpu.VMEM((NZ, 64, 1024), BF16),
             pltpu.VMEM((1024, 1024), BF16),
@@ -589,7 +656,7 @@
             *dma(3), *dma(3), *dma(3),
             *dma(8, CHUNKS), *dma(7, CHUNKS),
             *dma(NS - 1, 4), *dma(NS - 1), *dma(NS - 1),
-            *dma(9), *dma(NS - 1), *dma(NZ - 1), *dma(NZ - 1),
+            *dma(9), *dma(NS - 1), *dma(NZ - 1, 4), *dma(NZ - 1, 2),
             *dma(NS - 1), *dma(NZ - 1), *dma(NS - 1), *dma(3),
             *dma(8, CHUNKS), *dma(7, CHUNKS), *dma(8, CHUNKS), *dma(7, CHUNKS),
         ],
@@ -603,21 +670,21 @@
 
 
 def head_maps(old_heads, new_heads, member):
-    both = jnp.stack([old_heads, new_heads]).reshape(2, NZ, NS)
-    mine = lax.dynamic_index_in_dim(both, member, 1, keepdims=False)
+    both = lax.optimization_barrier(jnp.stack([old_heads, new_heads]))
+    mine = lax.dynamic_slice_in_dim(both, member * NS, NS, 1)
     groups = mine[0] // GROUP_HEADS
     j = jnp.arange(4, dtype=jnp.int32)
     block = 8 * (j // 2) + 2 * groups[:, None] + j % 2
     reads = (4 * (block % 4) + block // 4).reshape(4 * NS)
     slots = jnp.arange(NS, dtype=jnp.int32)
-    devices = jnp.arange(NZ, dtype=jnp.int32)
+    owner = jnp.arange(NZ * NS, dtype=jnp.int32) // NS
+    there = owner == jnp.arange(NZ, dtype=jnp.int32)[:, None]
+    moved = both[1][:, None] == mine[0]
     leaving = jnp.sum(
-        jnp.where(both[1][:, :, None] == mine[0], slots, 0), axis=(1, 2), dtype=jnp.int32
+        jnp.where(there[:, :, None] & moved, slots, 0), axis=(1, 2), dtype=jnp.int32
     )
     origin = jnp.sum(
-        jnp.where(both[0][:, :, None] == mine[1], devices[:, None, None], 0),
-        axis=(0, 1),
-        dtype=jnp.int32,
+        jnp.where(both[0] == mine[1][:, None], owner, 0), axis=1, dtype=jnp.int32
     )
     return groups, reads, leaving, origin
 

time: 227 us -> 214 us (0.943)
  Pallas kernels: 208 us -> 198 us
  local copies, waits for them, and re-layouts: 15 us -> 11.9 us
    pallas_call x1, Pallas kernels: 208 us -> 198 us  [layer_call(): pl.pallas_call(layer_kernel, out_shape=(jax.ShapeDtypeStruct((NZ, 64, 102...]
where the time goes in v3:
time: 214 us; the launch traced here: 213 us
  Pallas kernels  198 us (93%)
  local copies, waits for them, and re-layouts  11.9 us (6%)
  other arithmetic  2.2 us (1%)
    pallas_call x1, Pallas kernels, layer_call(): pl.pallas_call(layer_kernel, out_shape=(jax.ShapeDtypeStruct((NZ, 64, 102...  198 us
    unnamed x13, local copies, waits for them, and re-layouts  6.66 us

profile of v3, /device:TPU:6, one launch (start us, length us, event | category | flops | bytes accessed | tf_op | source)
XLA Modules:
  0.0 213.0 jit_solution(10063904090090013152)
XLA Ops:
  0.6 0.8 maximum_convert_fusion.scalars_ref
  1.4 0.7 pad_add_fusion
  2.1 0.1 constant_dynamic-slice_fusion
  2.2 0.2 select_reduce_fusion.1.origin_ref
  2.4 0.1 broadcast_compare_fusion
  2.5 0.4 select_reduce_fusion.leaving_ref
  2.8 0.1 add_add_fusion
  2.9 0.1 add.77
  3.0 0.7 pad.4.dt_ref
  3.7 0.9 copy.22
  4.6 1.1 copy.27
  5.8 0.0 copy-start
  5.8 0.9 copy-done
  6.7 0.0 copy-start.1
  6.7 0.9 copy-done.1
  7.7 0.0 copy-start.2
  7.7 0.7 copy-done.2
  8.4 0.0 copy-start.3
  8.4 0.7 copy-done.3
  9.0 0.0 copy-start.4
  9.0 0.7 copy-done.4
  9.7 198.2 %shard_map.148 = (bf16[16,64,1024]{2,1,0:T(8,128)(2,1)S(1)}, bf16[256,1024]{1,0:T(8,128)(2,1)S(1)}, bf16[512,256]{1,0:T(8,128)(2,1)S(1)}) custom-call(s32[8]{0:T(128)S(1)} %get-tuple-element.10.groups_ref, s32[32]{0:T(128)S(1)} %fusion.2.reads_ref, s32[16]{0:T(128)S(1)} %select_reduce_fusion.leaving_ref, s32[8]{0:T(128)S(1)} %select_reduce_fusion.1.origin_ref, ...), custom_call_target="tpu_custom_call" | custom-call | flops 4000000000 | bytes 100000000 | tf_op jit(solution)/shard_map/pallas_call | solution.py:610
  207.9 3.5 %copy.24 = bf16[16,32,2,1024]{3,2,1,0:T(2,128)(2,1)} copy(bf16[16,32,2,1024]{3,1,2,0:T(8,128)(2,1)S(1)} %bitcast.26) | data formatting | bytes 4194304 | tf_op jit(solution)/shard_map/transpose | solution.py:724
  211.4 0.9 copy.25
  212.3 0.7 copy.29
  (7 shorter events, 0.0 us)
Async XLA Ops:
  5.8 1.0 copy-start
  6.7 0.9 copy-start.1
  7.7 0.7 copy-start.2
  8.4 0.7 copy-start.3
  9.0 0.7 copy-start.4

commit v4 on v3

--- a/solution.py
+++ b/solution.py
@@ -55,9 +55,9 @@
 
 def layer_kernel(
     groups_ref, reads_ref, leaving_ref, origin_ref, scalars_ref,
-    act_ref, xz_ref, dt_ref, bc_hbm, out_hbm, group_taps_hbm, head_taps_hbm, gain_hbm,
+    act_ref, xz_ref, dt_ref, bc_hbm, out_hbm, head_taps_hbm, gain_hbm,
     mixed_out, new_xz, new_rows,
-    bc_ref, out_ref, group_taps_ref, head_taps_ref, gain_ref, load_sem,
+    bc_ref, out_ref, head_taps_ref, gain_ref, load_sem,
     hot_ref, acts, weights, dts, rows_all, parts, parts_in, bc_parts, bc_in, step_parts, steps_in,
     bc_all, chosen, groups_in, xz_leaving, xz_coming, rows_leaving, rows_coming,
     own_gated, gathered, own_squares, squares_in, squares, z_squares, totals, product,
@@ -79,7 +79,6 @@
             (
                 (out_hbm, out_ref),
                 (bc_hbm, bc_ref),
-                (group_taps_hbm, group_taps_ref),
                 (head_taps_hbm, head_taps_ref),
                 (gain_hbm, gain_ref),
             )
@@ -298,7 +297,7 @@
     for k in range(NS - 1):
         total = total + bc_in[k].astype(F32)
     own_class, own_turn = 4 * lax.rem(t, 4), t // 4
-    taps = group_taps_ref[...].astype(F32)
+    taps = dt_ref[8:16, 0:128].astype(F32)
     for m in range(2):
         rows = total[:, 32 * m : 32 * m + 32, :].reshape(96, 128)
         u = jnp.zeros((64, 128), F32)
@@ -614,15 +613,14 @@
             jax.ShapeDtypeStruct((256, 1024), BF16),
             jax.ShapeDtypeStruct((512, 256), BF16),
         ),
-        in_specs=[SMEM] * 5 + [VMEM] * 3 + [HBM] * 5,
+        in_specs=[SMEM] * 5 + [VMEM] * 3 + [HBM] * 4,
         out_specs=(VMEM,) * 3,
         scratch_shapes=[
             pltpu.VMEM((1024, 128), BF16),
             pltpu.VMEM((NS, 64, 256), BF16),
-            pltpu.VMEM((KERNEL, 128), BF16),
             pltpu.VMEM((NS, KERNEL, 64), BF16),
             pltpu.VMEM((NS, 64), BF16),
-            pltpu.SemaphoreType.DMA((5,)),
+            pltpu.SemaphoreType.DMA((4,)),
             pltpu.VMEM((16, 1024), BF16),
             pltpu.VMEM((NZ, 64, 1024), BF16),
             pltpu.VMEM((1024, 1024), BF16),
@@ -714,10 +712,11 @@
         jnp.concatenate([decay_log, dt_bias, skip_gain]).astype(F32),
         jnp.transpose(activations, (1, 0, 2)).reshape(64, 1024),
         jnp.transpose(xz_weight, (1, 0, 2)),
-        jnp.pad(jnp.transpose(dt_weight), ((0, 8), (0, 0))),
+        jnp.concatenate(
+            [jnp.transpose(dt_weight), jnp.pad(conv_groups, ((0, 4), (0, 128)))], axis=0
+        ),
         bc_weight,
         out_weight,
-        conv_groups,
         conv_heads,
         norm_gain,
     )

time: 214 us -> 213 us (level)
    unnamed x13 -> x11, local copies, waits for them, and re-layouts: 6.66 us -> 5.98 us
where the time goes in v4:
time: 213 us
  Pallas kernels  199 us (93%)
  local copies, waits for them, and re-layouts  10.6 us (5%)
  other arithmetic  2.91 us (1%)
    pallas_call x1, Pallas kernels, layer_call(): pl.pallas_call(layer_kernel, out_shape=(jax.ShapeDtypeStruct((NZ, 64, 102...  199 us
    unnamed x11, local copies, waits for them, and re-layouts  5.98 us

profile of v4, /device:TPU:6, one launch (start us, length us, event | category | flops | bytes accessed | tf_op | source)
XLA Modules:
  0.0 212.9 jit_solution(9371469214360594028)
XLA Ops:
  0.6 0.8 maximum_convert_fusion.scalars_ref
  1.4 0.7 pad_add_fusion
  2.1 0.1 constant_dynamic-slice_fusion
  2.2 0.2 select_reduce_fusion.1.origin_ref
  2.4 0.1 broadcast_compare_fusion
  2.5 0.4 select_reduce_fusion.leaving_ref
  2.8 0.1 add_add_fusion
  2.9 0.1 add.77
  3.0 0.7 fusion.1.dt_ref
  3.7 0.9 copy.22
  4.7 1.1 copy.27
  5.8 0.0 copy-start
  5.8 0.9 copy-done
  6.7 0.0 copy-start.1
  6.7 0.9 copy-done.1
  7.7 0.0 copy-start.2
  7.7 0.7 copy-done.2
  8.4 0.0 copy-start.3
  8.4 0.7 copy-done.3
  9.1 198.8 %shard_map.148 = (bf16[16,64,1024]{2,1,0:T(8,128)(2,1)S(1)}, bf16[256,1024]{1,0:T(8,128)(2,1)S(1)}, bf16[512,256]{1,0:T(8,128)(2,1)S(1)}) custom-call(s32[8]{0:T(128)S(1)} %get-tuple-element.10.groups_ref, s32[32]{0:T(128)S(1)} %fusion.4.reads_ref, s32[16]{0:T(128)S(1)} %select_reduce_fusion.leaving_ref, s32[8]{0:T(128)S(1)} %select_reduce_fusion.1.origin_ref, ...), custom_call_target="tpu_custom_call" | custom-call | flops 4000000000 | bytes 100000000 | tf_op jit(solution)/shard_map/pallas_call | solution.py:609
  207.9 3.5 %copy.24 = bf16[16,32,2,1024]{3,2,1,0:T(2,128)(2,1)} copy(bf16[16,32,2,1024]{3,1,2,0:T(8,128)(2,1)S(1)} %bitcast.26) | data formatting | bytes 4194304 | tf_op jit(solution)/shard_map/transpose | solution.py:723
  211.3 0.9 copy.25
  212.2 0.7 copy.29
  (7 shorter events, 0.0 us)
Async XLA Ops:
  5.8 1.0 copy-start
  6.7 0.9 copy-start.1
  7.7 0.7 copy-start.2
  8.4 0.7 copy-start.3
